TPU v7x, 32 devices: a whole 2x2x4 slice. The times are simulated.
32 devices in a mesh: seg: 8 (over z, core), chan: 4 (over y, x).
Axes of the slice: x: 2, y: 2, z: 4, core: 2. Of those that a mesh axis runs over, the one named last changes fastest.
Arguments:
- signal: bfloat16 [4096, 16384], P('chan', 'seg'), may hold values from -64 to 64
- spatial: float32 [4096, 64], P('chan'), may hold values from -0.09375 to 0.09375
- temporal: float32 [64, 256], replicated, may hold values from -5 to 5
- start_codes: float32 [64, 16384], P(None, 'seg'), may hold values from -1.2 to 1.2
- thresholds: float32 [64], replicated, may hold values from 0.05 to 0.3
- step_sizes: float32 [64], replicated, may hold values from 0.03 to 0.1
- breaks: int32 [16], replicated, may hold values from 0 to 16383, as said below
Outputs:
- final_codes: float32 [64, 16384], P(None, 'seg')
- space_atoms: float32 [4096, 64], P('chan')
- time_atoms: float32 [64, 256], replicated
Inputs may be any that keep to these rules, and one draw needn't show every extreme that they name: `breaks`: Increasing; one break lies in each of the 16 equal stretches of the window.
All inputs are finite; a program needn't handle non-finite values.
Results may differ from a plain program's by a relative error of at most 0.0058.
Values may be sent and summed in bfloat16 or wider, within the bound.
A program may use at most 128 MiB of HBM per device.

v0:
```python
import jax
import jax.numpy as jnp
from jax import lax
from jax.sharding import PartitionSpec as P

ITERS = 10
OUTER = 2


epsilon = 1e-06
highest = lax.Precision.HIGHEST


def passed_along(value, axis, steps):
    count = lax.axis_size(axis)
    leading, last = (max(0, -steps), min(count, count - steps))
    return lax.ppermute(value, axis, [(source, source + steps) for source in range(leading, last)])


def skewed(padded, row_total):
    atoms_here, period = padded.shape
    repeated = jnp.broadcast_to(padded[:, None, :], (atoms_here, row_total, period))
    flattened = repeated.reshape(atoms_here, row_total * period)[:, : row_total * (period - 1)]
    return flattened.reshape(atoms_here, row_total, period - 1)[:, :, :row_total]


def toeplitz(kernel_taps, block_width):
    atoms_here, tap_count = kernel_taps.shape
    zero_pad = jnp.zeros((atoms_here, block_width), kernel_taps.dtype)
    padded = jnp.concatenate([zero_pad, kernel_taps, zero_pad], axis=1)
    matrices = []
    for offset in range(tap_count // block_width + 1):
        earlier = padded[:, offset * block_width : (offset + 1) * block_width]
        current = padded[:, (offset + 1) * block_width : (offset + 2) * block_width]
        matrices.append(skewed(jnp.concatenate([current, earlier], axis=1), block_width))
    return matrices


def convolve_blocks(matrices, code_rows, before, block_width):
    atoms_here, seg_len = code_rows.shape
    block_count = seg_len // block_width
    lag_blocks = len(matrices) - 1
    extended = jnp.concatenate([before, code_rows], axis=1).reshape(
        atoms_here, block_count + lag_blocks, block_width
    )
    summed = jnp.zeros((atoms_here, block_count, block_width), jnp.float32)
    for offset, matrix in enumerate(matrices):
        window = extended[:, lag_blocks - offset : lag_blocks - offset + block_count]
        summed = summed + jnp.einsum(
            "kbm,kmi->kbi", window, matrix, preferred_element_type=jnp.float32, precision=highest
        )
    return summed.reshape(atoms_here, seg_len)


def correlate_blocks(matrices, residual_b, after_rim, block_width):
    atoms_here, seg_len = residual_b.shape
    block_count = seg_len // block_width
    extended = jnp.concatenate([residual_b, after_rim], axis=1).reshape(
        atoms_here, block_count + len(matrices) - 1, block_width
    )
    summed = jnp.zeros((atoms_here, block_count, block_width), jnp.float32)
    for offset, matrix in enumerate(matrices):
        window = extended[:, offset : offset + block_count]
        summed = summed + jnp.einsum(
            "kbi,kmi->kbm", window, matrix, preferred_element_type=jnp.float32, precision=highest
        )
    return summed.reshape(atoms_here, seg_len)


def reconstruct(matrices, latent_rows, block_width, tap_count):
    latent_b = latent_rows.astype(jnp.bfloat16)
    before = passed_along(latent_b[:, latent_b.shape[1] - tap_count :], "seg", 1)
    return (convolve_blocks(matrices, latent_b, before, block_width), before)


def on_device(signal, spatial, temporal, start_codes, thresholds, step_sizes, breaks):
    chan_rows, seg_len = signal.shape
    atoms_all, tap_count = temporal.shape
    block_width = 128
    positions = lax.axis_index("seg") * seg_len + lax.iota(jnp.int32, seg_len)
    crosses = (positions[None, :] < breaks[:, None]) & (
        breaks[:, None] < positions[None, :] + tap_count
    )
    allowed = jnp.where(jnp.any(crosses, axis=0), 0.0, 1.0).astype(jnp.float32)
    raw_start = lax.psum(jnp.dot(spatial.T, spatial, precision=highest), "chan")
    scaling = 1.0 / jnp.sqrt(jnp.diag(raw_start) + epsilon)
    space_loc = spatial * scaling[None, :]
    gram_matrix = raw_start * scaling[:, None] * scaling[None, :]
    kernel = temporal / jnp.sqrt(jnp.sum(temporal * temporal, axis=1, keepdims=True) + epsilon)
    latent = start_codes
    rows_share = chan_rows // lax.axis_size("seg")
    for sweep_index in range(OUTER):
        space_b = space_loc.astype(jnp.bfloat16)
        kernel_b = kernel.astype(jnp.bfloat16)
        projected = lax.psum(jnp.dot(space_b.T, signal, preferred_element_type=jnp.float32), "chan")
        own_gram = gram_matrix
        own_latent = latent

        def mix_atoms(rebuilt_part):
            return jnp.dot(own_gram, rebuilt_part, precision=highest)

        matrices = toeplitz(kernel_b, block_width)
        step_col = step_sizes[:, None]
        limit_col = (step_sizes * thresholds)[:, None]

        def shrink_step(iteration, current):
            rebuilt, before_now = reconstruct(matrices, current, block_width, tap_count)
            residual = projected - mix_atoms(rebuilt)
            residual_b = residual.astype(jnp.bfloat16)
            after_rim = passed_along(residual_b[:, :tap_count], "seg", -1)
            descent = correlate_blocks(matrices, residual_b, after_rim, block_width)
            stepped = current + step_col * descent
            return (
                allowed[None, :]
                * jnp.sign(stepped)
                * jnp.maximum(jnp.abs(stepped) - limit_col, 0.0)
            )

        own_latent = lax.fori_loop(0, ITERS, shrink_step, own_latent)
        rebuilt, before = reconstruct(matrices, own_latent, block_width, tap_count)
        latent = own_latent
        latent_b = latent.astype(jnp.bfloat16)
        rebuilt_b = rebuilt.astype(jnp.bfloat16)
        stats_rows = lax.psum_scatter(
            jnp.dot(signal, rebuilt_b.T, preferred_element_type=jnp.float32),
            "seg",
            scatter_dimension=0,
            tiled=True,
        )
        others = projected - jnp.dot(
            gram_matrix - jnp.diag(jnp.diag(gram_matrix)), rebuilt, precision=highest
        )

        def convolve_kernel(kernel_wide):
            return convolve_blocks(
                toeplitz(kernel_wide, block_width),
                latent_b.astype(jnp.float32),
                before.astype(jnp.float32),
                block_width,
            )

        primal, pullback = jax.vjp(convolve_kernel, kernel)
        (taps_part,) = pullback(others)
        cross_gram, raw_kernel = lax.psum(
            (jnp.dot(rebuilt, rebuilt.T, precision=highest), taps_part), "seg"
        )
        seg_first = lax.axis_index("seg") * rows_share
        own_space = lax.dynamic_slice_in_dim(space_loc, seg_first, rows_share, 0)
        raw_rows = stats_rows - jnp.dot(
            own_space, cross_gram - jnp.diag(jnp.diag(cross_gram)), precision=highest
        )
        squares = lax.psum(jnp.sum(raw_rows * raw_rows, axis=0), ("seg", "chan"))
        new_rows = raw_rows / jnp.sqrt(squares + epsilon)[None, :]
        space_loc = lax.all_gather(new_rows, "seg", axis=0, tiled=True)
        if sweep_index + 1 < OUTER:
            gram_matrix = lax.psum(jnp.dot(space_loc.T, space_loc, precision=highest), "chan")
        kernel = raw_kernel / jnp.sqrt(
            jnp.sum(raw_kernel * raw_kernel, axis=1, keepdims=True) + epsilon
        )
    return (latent, space_loc, kernel)


def solution(mesh):
    placed = (P("chan", "seg"), P("chan", None), P(), P(None, "seg"), P(), P(), P())
    return jax.shard_map(
        on_device,
        mesh=mesh,
        in_specs=placed,
        out_specs=(P(None, "seg"), P("chan", None), P()),
        check_vma=False,
    )
```

profile of v0, /device:TPU:25, one launch (start us, length us, event | category | flops | bytes accessed | tf_op | source)
XLA Modules:
  0.0 1027.2 jit_solution(3678279526802170328)
XLA Ops:
  8.7 12.5 %psum.70 = f32[64,64]{1,0:T(8,128)S(1)} all-reduce(f32[64,64]{1,0:T(8,128)S(1)} %fusion.98), channel_id=1, replica_groups=mesh['seg'=8,'chan'=4] {'chan'}, use_global_device_ids=true, to_apply=%region_1.2 | all-reduce | flops 4096 | bytes 32768 | tf_op jit(solution)/shard_map/psum | solution.py:85
  33.1 16.0 %reshape.190 = bf16[64,128,255]{2,1,0:T(8,128)(2,1)} reshape(bf16[64,32640]{1,0:T(8,128)(2,1)} %slice.200) | data formatting | bytes 8355840 | tf_op jit(solution)/shard_map/reshape | solution.py:24
  57.4 15.8 %reshape.192 = bf16[64,128,255]{2,1,0:T(8,128)(2,1)} reshape(bf16[64,32640]{1,0:T(8,128)(2,1)} %slice.204) | data formatting | bytes 8355840 | tf_op jit(solution)/shard_map/reshape | solution.py:24
  78.4 16.0 %reshape.194 = bf16[64,128,255]{2,1,0:T(8,128)(2,1)} reshape(bf16[64,32640]{1,0:T(8,128)(2,1)} %slice.206) | data formatting | bytes 8355840 | tf_op jit(solution)/shard_map/reshape | solution.py:24
  98.0 197.7 %while.20 = (s32[]{:T(128)}, f32[64,2048]{1,0:T(8,128)S(1)}, f32[2048]{0:T(1024)S(1)}, f32[64,1]{0,1:T(1,128)S(1)}, bf16[64,128,128]{2,1,0:T(8,128)(2,1)}, /*ind...) while((s32[]{:T(128)}, f32[64,2048]{1,0:T(8,128)S(1)}, ...), condition=%wide.region_5.6_spmd, body=%wide.region_4.5_spmd.sunk | while | flops 305135616 | bytes 44720912 | solution.py:119
  99.4 5.7 collective-permute-done
  129.2 4.5 collective-permute-start.1
  187.4 4.5 collective-permute-start.1
  318.2 6.5 pad.84
  324.7 9.3 reshape.203
  347.0 9.4 reshape.201
  369.5 9.3 reshape.199
  388.5 25.3 %psum.73 = f32[64,64]{1,0:T(8,128)S(1)} all-reduce(f32[64,64]{1,0:T(8,128)S(1)} %convolution_bitcast_fusion.5), channel_id=1, replica_groups=mesh['seg'=8,'chan'=4] {'seg'}, use_global_device_ids=true, to_apply=%region_12.13 | all-reduce | flops 4096 | bytes 32768 | tf_op jit(solution)/shard_map/psum | solution.py:144
  414.7 25.4 %all-reduce.33.cloned.1.call-done = f32[64,256]{1,0:T(8,128)} async-done(((f32[64,256]{1,0:T(8,128)}), f32[64,256]{1,0:T(8,128)}) %all-reduce.33.cloned.1.call-update) | async-done | bytes 65552 | tf_op jit(solution)/shard_map/psum | solution.py:144
  447.1 15.8 %reshape.206 = bf16[64,128,255]{2,1,0:T(8,128)(2,1)} reshape(bf16[64,32640]{1,0:T(8,128)(2,1)} %slice.211) | data formatting | bytes 8355840 | tf_op jit(solution)/shard_map/reshape | solution.py:24
  466.1 6.3 reduce-scatter.3.cloned.1.call-done
  473.5 38.5 %psum.74 = f32[64]{0:T(128)S(1)} all-reduce(f32[64]{0:T(128)S(1)} %get-tuple-element.173), channel_id=1, replica_groups=mesh['seg'=8,'chan'=4] {'seg','chan'}, use_global_device_ids=true, to_apply=%region_14.15 | all-reduce | flops 64 | bytes 512 | tf_op jit(solution)/shard_map/psum | solution.py:152
  512.2 16.1 %all_gather.6 = f32[1024,64]{0,1:T(8,128)S(1)} all-gather(f32[128,64]{0,1:T(8,128)S(1)} %broadcast_divide_fusion.2), channel_id=1, replica_groups=mesh['seg'=8,'chan'=4] {'seg'}, dimensions={0}, use_global_device_ids=true | all-gather | bytes 294912 | tf_op jit(solution)/shard_map/all_gather | solution.py:154
  537.9 16.0 %reshape.208 = bf16[64,128,255]{2,1,0:T(8,128)(2,1)} reshape(bf16[64,32640]{1,0:T(8,128)(2,1)} %slice.215) | data formatting | bytes 8355840 | tf_op jit(solution)/shard_map/reshape | solution.py:24
  559.0 15.8 %reshape.210 = bf16[64,128,255]{2,1,0:T(8,128)(2,1)} reshape(bf16[64,32640]{1,0:T(8,128)(2,1)} %slice.217) | data formatting | bytes 8355840 | tf_op jit(solution)/shard_map/reshape | solution.py:24
  578.5 12.8 %psum.75 = f32[64,64]{1,0:T(8,128)S(1)} all-reduce(f32[64,64]{1,0:T(8,128)S(1)} %fusion.99), channel_id=1, replica_groups=mesh['seg'=8,'chan'=4] {'chan'}, use_global_device_ids=true, to_apply=%region_15.16 | all-reduce | flops 4096 | bytes 32768 | tf_op jit(solution)/shard_map/psum | solution.py:156
  591.4 196.9 %while.21 = (s32[]{:T(128)}, f32[64,2048]{1,0:T(8,128)S(1)}, f32[2048]{0:T(1024)S(1)}, f32[64,1]{0,1:T(1,128)S(1)}, bf16[64,128,128]{2,1,0:T(8,128)(2,1)}, /*ind...) while((s32[]{:T(128)}, f32[64,2048]{1,0:T(8,128)S(1)}, ...), condition=%wide.region_18.19_spmd, body=%wide.region_17.18_spmd.sunk | while | flops 305135616 | bytes 44720912 | solution.py:119
  592.7 4.9 collective-permute-done.2
  621.8 4.5 collective-permute-start.3
  815.1 9.3 reshape.219
  837.4 9.5 reshape.217
  859.9 9.3 reshape.215
  878.7 25.3 %psum.77 = f32[64,64]{1,0:T(8,128)S(1)} all-reduce(f32[64,64]{1,0:T(8,128)S(1)} %convolution_bitcast_fusion.4), channel_id=1, replica_groups=mesh['seg'=8,'chan'=4] {'seg'}, use_global_device_ids=true, to_apply=%region_20.21 | all-reduce | flops 4096 | bytes 32768 | tf_op jit(solution)/shard_map/psum | solution.py:144
  904.8 26.3 %all-reduce.37.cloned.1.call-done = f32[64,256]{1,0:T(8,128)} async-done(((f32[64,256]{1,0:T(8,128)}), f32[64,256]{1,0:T(8,128)}) %all-reduce.37.cloned.1.call-update) | async-done | bytes 65552 | tf_op jit(solution)/shard_map/psum | solution.py:144
  933.6 29.7 %reduce-scatter.5.cloned.1.call-done = f32[128,64]{0,1:T(8,128)} async-done(((f32[1024,64]{0,1:T(8,128)}), f32[128,64]{0,1:T(8,128)}) %reduce-scatter.5.cloned.1.call-update) | async-done | bytes 32784 | tf_op jit(solution)/shard_map/reduce_scatter | solution.py:124
  964.4 38.5 %psum.78 = f32[64]{0:T(128)S(1)} all-reduce(f32[64]{0:T(128)S(1)} %get-tuple-element.175), channel_id=1, replica_groups=mesh['seg'=8,'chan'=4] {'seg','chan'}, use_global_device_ids=true, to_apply=%region_22.23 | all-reduce | flops 64 | bytes 512 | tf_op jit(solution)/shard_map/psum | solution.py:152
  1003.1 16.1 %all_gather.7 = f32[1024,64]{0,1:T(8,128)S(1)} all-gather(f32[128,64]{0,1:T(8,128)S(1)} %broadcast_divide_fusion.1), channel_id=1, replica_groups=mesh['seg'=8,'chan'=4] {'seg'}, dimensions={0}, use_global_device_ids=true | all-gather | bytes 294912 | tf_op jit(solution)/shard_map/all_gather | solution.py:154
  (671 shorter events, 554.6 us)
Async XLA Ops:
  7.2 90.8 %all-reduce.31.cloned.1.call-start = ((), (), s32[]{:S(2)}) async-start(), calls=%async_computation.2 | async-start | bytes 1048576 | tf_op jit(solution)/shard_map/psum | solution.py:95
  27.6 412.4 %all-reduce.33.cloned.1.call-start = ((), (), s32[]{:S(2)}) async-start(), calls=%async_computation.3 | async-start | bytes 131072 | tf_op jit(solution)/shard_map/psum | solution.py:144
  98.1 7.0 collective-permute-start
  109.8 5.4 collective-permute-start.1
  129.2 5.4 collective-permute-start.1
  148.6 5.4 collective-permute-start.1
  168.0 5.4 collective-permute-start.1
  187.4 5.4 collective-permute-start.1
  206.8 5.4 collective-permute-start.1
  226.2 5.4 collective-permute-start.1
  237.6 3.4 collective-permute-start
  245.6 5.4 collective-permute-start.1
  265.0 5.4 collective-permute-start.1
  284.4 5.4 collective-permute-start.1
  387.7 84.6 %reduce-scatter.3.cloned.1.call-start = ((), (), s32[]{:S(2)}) async-start(), calls=%async_computation.4 | async-start | bytes 294912 | tf_op jit(solution)/shard_map/reduce_scatter | solution.py:124
  414.6 176.7 %all-reduce.35.cloned.1.call-start = ((), (), s32[]{:S(2)}) async-start(), calls=%async_computation.5 | async-start | bytes 1048576 | tf_op jit(solution)/shard_map/psum | solution.py:95
  532.2 398.8 %all-reduce.37.cloned.1.call-start = ((), (), s32[]{:S(2)}) async-start(), calls=%async_computation.7 | async-start | bytes 131072 | tf_op jit(solution)/shard_map/psum | solution.py:144
  591.4 6.2 collective-permute-start.2
  602.4 5.4 collective-permute-start.3
  621.8 5.4 collective-permute-start.3
  641.2 5.4 collective-permute-start.3
  660.6 5.4 collective-permute-start.3
  680.0 5.4 collective-permute-start.3
  691.3 3.4 collective-permute-start.2
  699.4 5.4 collective-permute-start.3
  718.8 5.4 collective-permute-start.3
  738.2 5.4 collective-permute-start.3
  757.6 5.4 collective-permute-start.3
  768.9 3.4 collective-permute-start.2
  777.0 5.4 collective-permute-start.3
  788.3 3.4 collective-permute-start.5
  877.9 85.3 %reduce-scatter.5.cloned.1.call-start = ((), (), s32[]{:S(2)}) async-start(), calls=%async_computation.6 | async-start | bytes 294912 | tf_op jit(solution)/shard_map/reduce_scatter | solution.py:124
  (96 other events, 487.0 us)
Sparse Core Ops, SparseCore 0:
  27.8 48.0 all-reduce.30
  387.8 52.1 all-reduce.32
  442.9 29.3 reduce-scatter.2
  532.4 45.4 all-reduce.34
  878.1 52.9 all-reduce.36
  933.8 29.3 reduce-scatter.4
where the time goes:
time: 1040 us; the launch traced here: 1030 us
  local copies, waits for them, and re-layouts  278 us (27%)
  matrix products  244 us (23%)
  blocking collectives  185 us (18%)
  waiting for transfers between devices  155 us (15%)
  starting transfers between devices  120 us (12%)
  other arithmetic  27.5 us (3%)
  between operations  15.3 us (1%)
    reshape x12, local copies, waits for them, and re-layouts, skewed(): flattened.reshape(atoms_here, row_total, period - 1)[:, :, :row_total]  151 us
    ppermute x42, starting transfers between devices, passed_along(): lax.ppermute(value, axis, [(source, source + steps) for source in range(l...  119 us
    dot_general x72, matrix products, convolve_blocks(): jnp.einsum('kbm,kmi->kbi', window, matrix, preferred_element_type=jnp.flo...  105 us
    dot_general x60, matrix products, correlate_blocks(): jnp.einsum('kbi,kmi->kbm', window, matrix, preferred_element_type=jnp.flo...  104 us
    psum x2, blocking collectives, on_device(): squares = lax.psum(jnp.sum(raw_rows * raw_rows, axis=0), ('seg', 'chan'))  77.1 us
    ppermute x42, waiting for transfers between devices, passed_along(): lax.ppermute(value, axis, [(source, source + steps) for source in range(l...  66.9 us
    psum x2, waiting for transfers between devices, on_device(): lax.psum((jnp.dot(rebuilt, rebuilt.T, precision=highest), taps_part), 'seg')  51.6 us
    psum x2, blocking collectives, on_device(): lax.psum((jnp.dot(rebuilt, rebuilt.T, precision=highest), taps_part), 'seg')  50.5 us
  transfers between devices with their start and end apart: 48, of which 46 were waited for; matrix products, arithmetic and copies ran while one was open for 15% of the time, Pallas kernels for 0%

commit v1 on v0

v1 whole, which is shorter than its diff:
```python
import functools
import jax
import jax.numpy as jnp
from jax import lax
from jax.experimental import pallas as pl
from jax.experimental.pallas import tpu as pltpu
from jax.sharding import PartitionSpec as P

ITERS = 10
OUTER = 2
LANES = 128
HALO = 12


epsilon = 1e-06
highest = lax.Precision.HIGHEST


def passed_along(value, axis, steps):
    count = lax.axis_size(axis)
    leading, last = (max(0, -steps), min(count, count - steps))
    return lax.ppermute(value, axis, [(source, source + steps) for source in range(leading, last)])


def split3(matrix):
    high = matrix.astype(jnp.bfloat16)
    low = (matrix - high.astype(jnp.float32)).astype(jnp.bfloat16)
    return jnp.concatenate([high, high, low], axis=1)


def steps_kernel(
    steps, last, atoms, blocks, own,
    step_ref, limit_ref, latent_in, proj_in, taps_ref, flipped_ref, gram_ref, plain_ref,
    allowed_ref, inside_ref,
    *rest,
):
    if last:
        latent_out, rebuilt_out, lags_out, latent, proj, mixed, forward, backward = rest
    else:
        latent_out, latent, proj, mixed, forward, backward = rest

    def spread(block, carry):
        rows = pl.ds(pl.multiple_of(block * atoms, atoms), atoms)
        columns = pl.ds(pl.multiple_of(block * LANES, LANES), LANES)
        latent[rows, :] = latent_in[:, columns]
        proj[rows, :] = proj_in[:, columns]
        return carry

    lax.fori_loop(0, blocks, spread, 0)

    def build(atom, carry):
        for source, target in ((taps_ref, forward), (flipped_ref, backward)):
            row = jnp.broadcast_to(source[pl.ds(atom, 1), :], (LANES, 4 * LANES))
            turned = pltpu.roll(row, 0, 1, stride=1, stride_axis=0).astype(jnp.bfloat16)
            for part in range(3):
                target[atom, part * LANES : (part + 1) * LANES, :] = turned[
                    :, part * LANES : (part + 1) * LANES
                ]
        return carry

    lax.fori_loop(0, atoms, build, 0)

    def rows_of(atom):
        return pl.ds(atom, blocks, stride=atoms)

    def window(values):
        return jnp.concatenate(
            [values, pltpu.roll(values, 1, 0), pltpu.roll(values, 2, 0)], axis=1
        ).astype(jnp.bfloat16)

    def convolve(atom, carry):
        mixed[rows_of(atom), :] = jnp.dot(
            window(latent[rows_of(atom), :]), forward[atom], preferred_element_type=jnp.float32
        )
        return carry

    def mix(block, carry, matrix_ref):
        rows = pl.ds(pl.multiple_of(block * atoms, atoms), atoms)
        rebuilt = mixed[rows, :]
        high = rebuilt.astype(jnp.bfloat16)
        low = (rebuilt - high.astype(jnp.float32)).astype(jnp.bfloat16)
        stacked = jnp.concatenate([high, low, high], axis=0)
        mixed[rows, :] = proj[rows, :] - jnp.dot(
            matrix_ref[...], stacked, preferred_element_type=jnp.float32
        )
        return carry

    def shrink(atom, carry):
        residual = jnp.where(inside_ref[...] > 0.5, mixed[rows_of(atom), :], 0.0)
        ahead = pltpu.roll(residual, blocks - 1, 0)
        further = pltpu.roll(residual, blocks - 2, 0)
        descent = jnp.dot(
            jnp.concatenate([further, ahead, residual], axis=1).astype(jnp.bfloat16),
            backward[atom],
            preferred_element_type=jnp.float32,
        )
        limit = limit_ref[atom]
        stepped = latent[rows_of(atom), :] + step_ref[atom] * descent
        latent[rows_of(atom), :] = allowed_ref[...] * (
            stepped - jnp.minimum(jnp.maximum(stepped, -limit), limit)
        )
        return carry

    def one_step(iteration, carry):
        lax.fori_loop(0, atoms, convolve, 0, unroll=8)
        lax.fori_loop(0, blocks, functools.partial(mix, matrix_ref=gram_ref), 0, unroll=4)
        lax.fori_loop(0, atoms, shrink, 0, unroll=8)
        return carry

    lax.fori_loop(0, steps, one_step, 0)
    for block in range(own):
        first = (HALO + block) * atoms
        latent_out[:, block * LANES : (block + 1) * LANES] = latent[first : first + atoms, :]
    if not last:
        return
    lax.fori_loop(0, atoms, convolve, 0, unroll=8)
    for block in range(own):
        first = (HALO + block) * atoms
        rebuilt_out[:, block * LANES : (block + 1) * LANES] = mixed[first : first + atoms, :]
    lax.fori_loop(HALO, HALO + own, functools.partial(mix, matrix_ref=plain_ref), 0, unroll=4)

    def lagged(atom, carry):
        codes = latent[rows_of(atom), :]
        codes = jnp.concatenate([pltpu.roll(codes, 2, 0), pltpu.roll(codes, 1, 0), codes], axis=1)
        codes = codes[HALO - 4 : HALO + own + 4]
        others = mixed[rows_of(atom), :][HALO - 4 : HALO + own + 4]
        place = lax.broadcasted_iota(jnp.int32, others.shape, 0)
        others = jnp.where((place >= 4) & (place < own + 4), others, 0.0)
        high = others.astype(jnp.bfloat16).astype(jnp.float32)
        pair = jnp.concatenate([high, others - high], axis=0).astype(jnp.bfloat16)
        twice = jnp.concatenate([codes, codes], axis=0).astype(jnp.bfloat16)
        total = lax.dot_general(
            pair, twice, (((0,), (0,)), ((), ())), preferred_element_type=jnp.float32
        )
        half = LANES // 2
        while half >= 1:
            total = total[:half] + pltpu.roll(total[half:], 3 * LANES - half, 1)
            half //= 2
        lags_out[pl.ds(atom, 1), :] = total
        return carry

    lax.fori_loop(0, atoms, lagged, 0, unroll=2)


def run_steps(steps, last, latent, projected, kernel_b, gram_matrix, step, limit, allowed, inside):
    atoms, width = latent.shape
    blocks = width // LANES
    own = blocks - 2 * HALO
    taps = kernel_b.astype(jnp.float32)
    tap_count = taps.shape[1]
    forward = jnp.pad(taps, ((0, 0), (0, 4 * LANES - tap_count)))
    backward = jnp.pad(taps[:, ::-1], ((0, 0), (1, 4 * LANES - tap_count - 1)))
    plain = gram_matrix - jnp.diag(jnp.diag(gram_matrix))
    out = [jax.ShapeDtypeStruct((atoms, own * LANES), jnp.float32)]
    if last:
        out.append(jax.ShapeDtypeStruct((atoms, own * LANES), jnp.float32))
        out.append(jax.ShapeDtypeStruct((atoms, 3 * LANES), jnp.float32))
    in_vmem = pl.BlockSpec(memory_space=pltpu.VMEM)
    in_smem = pl.BlockSpec(memory_space=pltpu.SMEM)
    return pl.pallas_call(
        functools.partial(steps_kernel, steps, last, atoms, blocks, own),
        out_shape=out,
        in_specs=[in_smem] * 2 + [in_vmem] * 8,
        out_specs=[in_vmem] * len(out),
        scratch_shapes=[pltpu.VMEM((blocks * atoms, LANES), jnp.float32)] * 3
        + [pltpu.VMEM((atoms, 3 * LANES, LANES), jnp.bfloat16)] * 2,
        compiler_params=pltpu.CompilerParams(vmem_limit_bytes=48 * 1024 * 1024),
        cost_estimate=pl.CostEstimate(
            flops=4 * steps * atoms * width * 3 * LANES, bytes_accessed=8 * atoms * width, transcendentals=0
        ),
    )(
        step, limit, latent, projected, forward, backward, split3(gram_matrix), split3(plain),
        allowed.reshape(blocks, LANES), inside.reshape(blocks, LANES),
    )


def widened(value):
    rim = HALO * LANES
    before = passed_along(value[:, value.shape[1] - rim :], "seg", 1)
    after = passed_along(value[:, :rim], "seg", -1)
    return jnp.concatenate([before, value, after], axis=1)


def on_device(signal, spatial, temporal, start_codes, thresholds, step_sizes, breaks):
    chan_rows, seg_len = signal.shape
    atoms_all, tap_count = temporal.shape
    rim = HALO * LANES
    positions = lax.axis_index("seg") * seg_len - rim + lax.iota(jnp.int32, seg_len + 2 * rim)
    inside = (positions >= 0) & (positions < seg_len * lax.axis_size("seg"))
    crosses = (positions[None, :] < breaks[:, None]) & (
        breaks[:, None] < positions[None, :] + tap_count
    )
    allowed = jnp.where(jnp.any(crosses, axis=0) | ~inside, 0.0, 1.0).astype(jnp.float32)
    inside = inside.astype(jnp.float32)
    raw_start = lax.psum(jnp.dot(spatial.T, spatial, precision=highest), "chan")
    scaling = 1.0 / jnp.sqrt(jnp.diag(raw_start) + epsilon)
    space_loc = spatial * scaling[None, :]
    gram_matrix = raw_start * scaling[:, None] * scaling[None, :]
    kernel = temporal / jnp.sqrt(jnp.sum(temporal * temporal, axis=1, keepdims=True) + epsilon)
    latent = start_codes
    limits = step_sizes * thresholds
    rows_share = chan_rows // lax.axis_size("seg")
    for sweep_index in range(OUTER):
        space_b = space_loc.astype(jnp.bfloat16)
        kernel_b = kernel.astype(jnp.bfloat16)
        projected = lax.psum(jnp.dot(space_b.T, signal, preferred_element_type=jnp.float32), "chan")
        wide = widened(projected)
        (latent,) = run_steps(
            ITERS // 2, False, widened(latent), wide, kernel_b, gram_matrix,
            step_sizes, limits, allowed, inside,
        )
        latent, rebuilt, lags = run_steps(
            ITERS - ITERS // 2, True, widened(latent), wide, kernel_b, gram_matrix,
            step_sizes, limits, allowed, inside,
        )
        taps_part = lags[:, 1 : tap_count + 1][:, ::-1]
        rebuilt_b = rebuilt.astype(jnp.bfloat16)
        stats_rows = lax.psum_scatter(
            jnp.dot(signal, rebuilt_b.T, preferred_element_type=jnp.float32),
            "seg",
            scatter_dimension=0,
            tiled=True,
        )
        summed = lax.psum(
            jnp.concatenate(
                [jnp.dot(rebuilt, rebuilt.T, precision=highest), taps_part], axis=1
            ),
            "seg",
        )
        cross_gram, raw_kernel = summed[:, :atoms_all], summed[:, atoms_all:]
        seg_first = lax.axis_index("seg") * rows_share
        own_space = lax.dynamic_slice_in_dim(space_loc, seg_first, rows_share, 0)
        raw_rows = stats_rows - jnp.dot(
            own_space, cross_gram - jnp.diag(jnp.diag(cross_gram)), precision=highest
        )
        squares = lax.psum(jnp.sum(raw_rows * raw_rows, axis=0), ("seg", "chan"))
        new_rows = raw_rows / jnp.sqrt(squares + epsilon)[None, :]
        space_loc = lax.all_gather(new_rows, "seg", axis=0, tiled=True)
        if sweep_index + 1 < OUTER:
            gram_matrix = lax.psum(jnp.dot(space_loc.T, space_loc, precision=highest), "chan")
        kernel = raw_kernel / jnp.sqrt(
            jnp.sum(raw_kernel * raw_kernel, axis=1, keepdims=True) + epsilon
        )
    return (latent, space_loc, kernel)


def solution(mesh):
    placed = (P("chan", "seg"), P("chan", None), P(), P(None, "seg"), P(), P(), P())
    return jax.shard_map(
        on_device,
        mesh=mesh,
        in_specs=placed,
        out_specs=(P(None, "seg"), P("chan", None), P()),
        check_vma=False,
    )
```

time: 1040 us -> 734 us (0.71)
  local copies, waits for them, and re-layouts: 278 us -> 11 us
  Pallas kernels: 0 us -> 265 us
  matrix products: 244 us -> 21.6 us
  starting transfers between devices: 120 us -> 48.3 us
  waiting for transfers between devices: 155 us -> 225 us
  blocking collectives: 185 us -> 135 us
  other arithmetic: 27.5 us -> 9.79 us
    pallas_call x0 -> x4, Pallas kernels: none -> 265 us  [run_steps(): pl.pallas_call(functools.partial(steps_kernel, steps, last, atoms, blocks...]
    dot_general x154 -> x0, matrix products: 226 us -> none  [the longest x72 105 us: convolve_blocks(): jnp.einsum('kbm,kmi->kbi', window, matrix, preferred_element_type=jnp.flo...]
    reshape x54 -> x0, local copies, waits for them, and re-layouts: 158 us -> none  [the longest x12 151 us: skewed(): flattened.reshape(atoms_here, row_total, period - 1)[:, :, :row_total]]
    ppermute x42 -> x12, starting transfers between devices: 119 us -> 48.1 us  [passed_along(): lax.ppermute(value, axis, [(source, source + steps) for source in range(l...]
    psum x2, waiting for transfers between devices: 0.02 us -> 68.6 us  [on_device(): lax.psum(jnp.dot(space_b.T, signal, preferred_element_type=jnp.float32),...]
    ppermute x42 -> x12, waiting for transfers between devices: 66.9 us -> 4.27 us  [passed_along(): lax.ppermute(value, axis, [(source, source + steps) for source in range(l...]
    pad x12 -> x4, local copies, waits for them, and re-layouts: 52.3 us -> 0.19 us  [the longest x2 0.16 us: run_steps(): backward = jnp.pad(taps[:, ::-1], ((0, 0), (1, 4 * LANES - tap_count - 1)))]
    psum x2 -> x0, blocking collectives: 50.5 us -> none  [on_device(): lax.psum((jnp.dot(rebuilt, rebuilt.T, precision=highest), taps_part), 'seg')]
  transfers between devices with their start and end apart: 48 -> 18, of which waited for: 46 -> 10; matrix products, arithmetic and copies ran while one was open for 15% -> 4% of each run, Pallas kernels for 0% -> 0%
where the time goes in v1:
time: 734 us; the launch traced here: 731 us
  Pallas kernels  265 us (36%)
  waiting for transfers between devices  225 us (31%)
  blocking collectives  135 us (18%)
  starting transfers between devices  48.3 us (7%)
  matrix products  21.6 us (3%)
  between operations  14.7 us (2%)
  local copies, waits for them, and re-layouts  11 us (1%)
  other arithmetic  9.79 us (1%)
    pallas_call x4, Pallas kernels, run_steps(): pl.pallas_call(functools.partial(steps_kernel, steps, last, atoms, blocks...  265 us
    psum x2, waiting for transfers between devices, on_device(): lax.psum(jnp.concatenate([jnp.dot(rebuilt, rebuilt.T, precision=highest),...  95.7 us
    psum x2, blocking collectives, on_device(): squares = lax.psum(jnp.sum(raw_rows * raw_rows, axis=0), ('seg', 'chan'))  77.1 us
    psum x2, waiting for transfers between devices, on_device(): lax.psum(jnp.dot(space_b.T, signal, preferred_element_type=jnp.float32),...  68.6 us
    reduce_scatter x2, waiting for transfers between devices, on_device(): lax.psum_scatter(jnp.dot(signal, rebuilt_b.T, preferred_element_type=jnp....  56.4 us
    ppermute x12, starting transfers between devices, passed_along(): lax.ppermute(value, axis, [(source, source + steps) for source in range(l...  48.1 us
    all_gather x2, blocking collectives, on_device(): space_loc = lax.all_gather(new_rows, 'seg', axis=0, tiled=True)  32.3 us
  transfers between devices with their start and end apart: 18, of which 10 were waited for; matrix products, arithmetic and copies ran while one was open for 4% of the time, Pallas kernels for 0%

profile of v1, /device:TPU:25, one launch (start us, length us, event | category | flops | bytes accessed | tf_op | source)
XLA Modules:
  0.0 730.5 jit_solution(17386805648890024658)
XLA Ops:
  7.2 1.4 fusion.37
  8.7 12.5 %psum.56 = f32[64,64]{1,0:T(8,128)S(1)} all-reduce(f32[64,64]{1,0:T(8,128)S(1)} %fusion.37), channel_id=1, replica_groups=mesh['seg'=8,'chan'=4] {'chan'}, use_global_device_ids=true, to_apply=%region_0.0 | all-reduce | flops 4096 | bytes 32768 | tf_op jit(solution)/shard_map/psum | solution.py:195
  22.1 3.9 fusion.4
  26.2 1.3 collective-permute-start
  27.5 7.0 collective-permute-start.1
  36.4 37.9 %all-reduce.9.cloned.1.call-done = f32[64,2048]{1,0:T(8,128)} async-done(((f32[64,2048]{1,0:T(8,128)}), f32[64,2048]{1,0:T(8,128)}) %all-reduce.9.cloned.1.call-update) | async-done | bytes 524304 | tf_op jit(solution)/shard_map/psum | solution.py:206
  75.4 1.4 collective-permute-start.2
  77.0 3.4 collective-permute-start.3
  81.8 52.3 %shard_map.94 = f32[64,2048]{1,0:T(8,128)S(1)} custom-call(f32[64]{0:T(128)S(1)} %copy-done, f32[64]{0:T(128)S(1)} %mul.49.limit_ref, f32[64,5120]{1,0:T(8,128)S(1)} %pad_maximum_fusion.latent_in, f32[64,5120]{1,0:T(8,128)S(1)} %constant_dynamic-update-slice_fusion.proj_in, f32[64,512]{1,0:T(8,128)S(1)} %pad.18.taps_ref, f32[64,512]{1,0:T(8,128)S(1)} %pad.19.flipped_ref, ...), custom_call_target="tpu_custom_call" | custom-call | flops 2516582400 | bytes 2621440 | tf_op jit(solution)/shard_map/pallas_call | solution.py:160
  136.1 9.0 %collective-permute-start.5 = (f32[64,1536]{1,0:T(8,128)S(1)}, f32[64,1536]{1,0:T(8,128)}, u32[]{:S(2)}, u32[]{:S(2)}) collective-permute-start(f32[64,1536]{1,0:T(8,128)S(1)} %get-tuple-element.27), channel_id=1, source_target_pairs={{4,0},{8,4},{12,8},{16,12},{20,16},{24,20},{28,24},{5,1},{9,5},{13... | collective-permute-start | bytes 1179656 | tf_op jit(solution)/shard_map/ppermute | solution.py:22
  146.9 80.4 %shard_map.95 = (f32[64,2048]{1,0:T(8,128)S(1)}, f32[64,2048]{1,0:T(8,128)S(1)}, f32[64,384]{1,0:T(8,128)S(1)}) custom-call(f32[64]{0:T(128)S(1)} %copy-done, f32[64]{0:T(128)S(1)} %mul.49.limit_ref, f32[64,5120]{1,0:T(8,128)S(1)} %pad_maximum_fusion.1.latent_in, f32[64,5120]{1,0:T(8,128)S(1)} %constant_dynamic-update-slice_fusion.proj_in, ...), custom_call_target="tpu_custom_call" | custom-call | flops 2516582400 | bytes 2621440 | tf_op jit(solution)/shard_map/pallas_call | solution.py:160
  229.1 4.3 convolution_bitcast_fusion.1
  234.7 9.0 %collective-permute-start.7 = (f32[64,1536]{1,0:T(8,128)S(1)}, f32[64,1536]{1,0:T(8,128)}, u32[]{:S(2)}, u32[]{:S(2)}) collective-permute-start(f32[64,1536]{1,0:T(8,128)S(1)} %get-tuple-element.25), channel_id=1, source_target_pairs={{4,0},{8,4},{12,8},{16,12},{20,16},{24,20},{28,24},{5,1},{9,5},{13... | collective-permute-start | bytes 1179656 | tf_op jit(solution)/shard_map/ppermute | solution.py:22
  243.7 42.8 %all-reduce.11.cloned.1.call-done = f32[64,320]{1,0:T(8,128)} async-done(((f32[64,320]{1,0:T(8,128)}), f32[64,320]{1,0:T(8,128)}) %all-reduce.11.cloned.1.call-update) | async-done | bytes 81936 | tf_op jit(solution)/shard_map/psum | solution.py:224
  290.4 28.4 %reduce-scatter.3.cloned.1.call-done = f32[128,64]{0,1:T(8,128)} async-done(((f32[1024,64]{0,1:T(8,128)}), f32[128,64]{0,1:T(8,128)}) %reduce-scatter.3.cloned.1.call-update) | async-done | bytes 32784 | tf_op jit(solution)/shard_map/reduce_scatter | solution.py:218
  320.1 38.6 %psum.59 = f32[64]{0:T(128)S(1)} all-reduce(f32[64]{0:T(128)S(1)} %get-tuple-element.38), channel_id=1, replica_groups=mesh['seg'=8,'chan'=4] {'seg','chan'}, use_global_device_ids=true, to_apply=%region_7.8 | all-reduce | flops 64 | bytes 512 | tf_op jit(solution)/shard_map/psum | solution.py:236
  358.7 16.1 %all_gather.6 = f32[1024,64]{0,1:T(8,128)S(1)} all-gather(f32[128,64]{0,1:T(8,128)S(1)} %broadcast_divide_fusion.1), channel_id=1, replica_groups=mesh['seg'=8,'chan'=4] {'seg'}, dimensions={0}, use_global_device_ids=true | all-gather | bytes 294912 | tf_op jit(solution)/shard_map/all_gather | solution.py:238
  374.9 3.8 fusion.2
  380.3 12.7 %psum.61 = f32[64,64]{1,0:T(8,128)S(1)} all-reduce(f32[64,64]{1,0:T(8,128)S(1)} %fusion.39), channel_id=1, replica_groups=mesh['seg'=8,'chan'=4] {'chan'}, use_global_device_ids=true, to_apply=%region_10.11 | all-reduce | flops 4096 | bytes 32768 | tf_op jit(solution)/shard_map/psum | solution.py:240
  393.8 30.7 %all-reduce.13.cloned.1.call-done = f32[64,2048]{1,0:T(8,128)} async-done(((f32[64,2048]{1,0:T(8,128)}), f32[64,2048]{1,0:T(8,128)}) %all-reduce.13.cloned.1.call-update) | async-done | bytes 524304 | tf_op jit(solution)/shard_map/psum | solution.py:206
  425.7 1.3 collective-permute-start.8
  427.3 3.6 collective-permute-start.9
  432.0 52.3 %shard_map.96 = f32[64,2048]{1,0:T(8,128)S(1)} custom-call(f32[64]{0:T(128)S(1)} %copy-done, f32[64]{0:T(128)S(1)} %mul.49.limit_ref, f32[64,5120]{1,0:T(8,128)S(1)} %pad_maximum_fusion.2.latent_in, f32[64,5120]{1,0:T(8,128)S(1)} %constant_dynamic-update-slice_fusion.3.proj_in, f32[64,512]{1,0:T(8,128)S(1)} %pad.20.taps_ref, f32[64,512]{1,0:T(8,128)S(1)} %pad.21.flipped_ref, ...), custom_call_target="tpu_custom_call" | custom-call | flops 2516582400 | bytes 2621440 | tf_op jit(solution)/shard_map/pallas_call | solution.py:160
  485.7 8.2 %collective-permute-start.11 = (f32[64,1536]{1,0:T(8,128)S(1)}, f32[64,1536]{1,0:T(8,128)S(1)}, u32[]{:S(2)}, u32[]{:S(2)}) collective-permute-start(f32[64,1536]{1,0:T(8,128)S(1)} %get-tuple-element.21), channel_id=1, source_target_pairs={{4,0},{8,4},{12,8},{16,12},{20,16},{24,20},{28,24},{5,1},{9,5},{13... | collective-permute-start | bytes 1179656 | tf_op jit(solution)/shard_map/ppermute | solution.py:22
  493.9 1.3 collective-permute-done.11
  495.3 80.5 %shard_map.97 = (f32[64,2048]{1,0:T(8,128)}, f32[64,2048]{1,0:T(8,128)S(1)}, f32[64,384]{1,0:T(8,128)S(1)}) custom-call(f32[64]{0:T(128)S(1)} %copy-done, f32[64]{0:T(128)S(1)} %mul.49.limit_ref, f32[64,5120]{1,0:T(8,128)S(1)} %pad_maximum_fusion.3.latent_in, f32[64,5120]{1,0:T(8,128)S(1)} %constant_dynamic-update-slice_fusion.3.proj_in, ...), custom_call_target="tpu_custom_call" | custom-call | flops 2516582400 | bytes 2621440 | tf_op jit(solution)/shard_map/pallas_call | solution.py:160
  577.5 4.3 convolution_bitcast_fusion
  581.8 53.0 %all-reduce.15.cloned.1.call-done = f32[64,320]{1,0:T(8,128)} async-done(((f32[64,320]{1,0:T(8,128)}), f32[64,320]{1,0:T(8,128)}) %all-reduce.15.cloned.1.call-update) | async-done | bytes 81936 | tf_op jit(solution)/shard_map/psum | solution.py:224
  637.4 1.6 slice_divide_fusion
  639.0 27.9 %reduce-scatter.5.cloned.1.call-done = f32[128,64]{0,1:T(8,128)} async-done(((f32[1024,64]{0,1:T(8,128)}), f32[128,64]{0,1:T(8,128)}) %reduce-scatter.5.cloned.1.call-update) | async-done | bytes 32784 | tf_op jit(solution)/shard_map/reduce_scatter | solution.py:218
  668.2 38.6 %psum.63 = f32[64]{0:T(128)S(1)} all-reduce(f32[64]{0:T(128)S(1)} %get-tuple-element.40), channel_id=1, replica_groups=mesh['seg'=8,'chan'=4] {'seg','chan'}, use_global_device_ids=true, to_apply=%region_14.15 | all-reduce | flops 64 | bytes 512 | tf_op jit(solution)/shard_map/psum | solution.py:236
  706.8 16.1 %all_gather.7 = f32[1024,64]{0,1:T(8,128)S(1)} all-gather(f32[128,64]{0,1:T(8,128)S(1)} %broadcast_divide_fusion), channel_id=1, replica_groups=mesh['seg'=8,'chan'=4] {'seg'}, dimensions={0}, use_global_device_ids=true | all-gather | bytes 294912 | tf_op jit(solution)/shard_map/all_gather | solution.py:238
  (109 shorter events, 30.2 us)
Async XLA Ops:
  7.2 14.9 %copy-start.4 = (f32[1024,64]{0,1:T(8,128)S(1)}, f32[1024,64]{0,1:T(8,128)}, u32[]{:S(2)}) copy-start(f32[1024,64]{0,1:T(8,128)} %param.8) | copy-start | bytes 786436
  7.2 67.1 %all-reduce.9.cloned.1.call-start = ((), (), s32[]{:S(2)}) async-start(), calls=%async_computation.2 | async-start | bytes 1048576 | tf_op jit(solution)/shard_map/psum | solution.py:206
  22.1 4.0 copy-start.1
  26.0 9.5 %copy-start.5 = (f32[64,256]{1,0:T(8,128)S(1)}, f32[64,256]{1,0:T(8,128)}, u32[]{:S(2)}) copy-start(f32[64,256]{1,0:T(8,128)} %param.9) | copy-start | bytes 196612
  26.1 10.0 %copy-start = (f32[64]{0:T(128)S(1)}, f32[64]{0:T(128)}, u32[]{:S(2)}) copy-start(f32[64]{0:T(128)} %step_ref.7) | copy-start | bytes 772
  26.1 10.0 %copy-start.7 = (f32[64]{0:T(128)S(1)}, f32[64]{0:T(128)}, u32[]{:S(2)}) copy-start(f32[64]{0:T(128)} %param.11) | copy-start | bytes 772
  26.1 10.1 %copy-start.6 = (s32[16]{0:T(128)S(1)}, s32[16]{0:T(128)}, u32[]{:S(2)}) copy-start(s32[16]{0:T(128)} %param.13) | copy-start | bytes 196
  26.1 260.4 %all-reduce.11.cloned.1.call-start = ((), (), s32[]{:S(2)}) async-start(), calls=%async_computation.4 | async-start | bytes 196608 | tf_op jit(solution)/shard_map/psum | solution.py:224
  26.2 50.6 %collective-permute-start = (f32[64,1536]{1,0:T(8,128)S(1)}, f32[64,1536]{1,0:T(8,128)S(1)}, u32[]{:S(2)}, u32[]{:S(2)}) collective-permute-start(f32[64,1536]{1,0:T(8,128)S(1)} %get-tuple-element.30), channel_id=1, source_target_pairs={{0,4},{4,8},{8,12},{12,16},{16,20},{20,24},{24,28},{1,5},{5,9},{9,... | collective-permute-start | bytes 1179656 | tf_op jit(solution)/shard_map/ppermute | solution.py:22
  27.5 49.3 %collective-permute-start.1 = (f32[64,1536]{1,0:T(8,128)S(1)}, f32[64,1536]{1,0:T(8,128)S(1)}, u32[]{:S(2)}, u32[]{:S(2)}) collective-permute-start(f32[64,1536]{1,0:T(8,128)S(1)} %get-tuple-element.31), channel_id=1, source_target_pairs={{4,0},{8,4},{12,8},{16,12},{20,16},{24,20},{28,24},{5,1},{9,5},{13... | collective-permute-start | bytes 1179656 | tf_op jit(solution)/shard_map/ppermute | solution.py:22
  75.4 5.0 copy-start.2
  75.4 5.0 collective-permute-start.2
  77.0 4.7 collective-permute-start.3
  134.9 10.3 %collective-permute-start.4 = (f32[64,1536]{1,0:T(8,128)}, f32[64,1536]{1,0:T(8,128)S(1)}, u32[]{:S(2)}, u32[]{:S(2)}) collective-permute-start(f32[64,1536]{1,0:T(8,128)} %get-tuple-element.26), channel_id=1, source_target_pairs={{0,4},{4,8},{8,12},{12,16},{16,20},{20,24},{24,28},{1,5},{5,9},{9,... | collective-permute-start | bytes 1179656 | tf_op jit(solution)/shard_map/ppermute | solution.py:22
  136.1 9.7 %collective-permute-start.5 = (f32[64,1536]{1,0:T(8,128)S(1)}, f32[64,1536]{1,0:T(8,128)}, u32[]{:S(2)}, u32[]{:S(2)}) collective-permute-start(f32[64,1536]{1,0:T(8,128)S(1)} %get-tuple-element.27), channel_id=1, source_target_pairs={{4,0},{8,4},{12,8},{16,12},{20,16},{24,20},{28,24},{5,1},{9,5},{13... | collective-permute-start | bytes 1179656 | tf_op jit(solution)/shard_map/ppermute | solution.py:22
  228.9 89.9 %reduce-scatter.3.cloned.1.call-start = ((), (), s32[]{:S(2)}) async-start(), calls=%async_computation.3 | async-start | bytes 294912 | tf_op jit(solution)/shard_map/reduce_scatter | solution.py:218
  233.4 145.4 %collective-permute-start.6 = (f32[64,1536]{1,0:T(8,128)S(1)}, f32[64,1536]{1,0:T(8,128)S(1)}, u32[]{:S(2)}, u32[]{:S(2)}) collective-permute-start(f32[64,1536]{1,0:T(8,128)S(1)} %get-tuple-element.24), channel_id=1, source_target_pairs={{0,4},{4,8},{8,12},{12,16},{16,20},{20,24},{24,28},{1,5},{5,9},{9,... | collective-permute-start | bytes 1179656 | tf_op jit(solution)/shard_map/ppermute | solution.py:22
  234.7 144.1 %collective-permute-start.7 = (f32[64,1536]{1,0:T(8,128)S(1)}, f32[64,1536]{1,0:T(8,128)}, u32[]{:S(2)}, u32[]{:S(2)}) collective-permute-start(f32[64,1536]{1,0:T(8,128)S(1)} %get-tuple-element.25), channel_id=1, source_target_pairs={{4,0},{8,4},{12,8},{16,12},{20,16},{24,20},{28,24},{5,1},{9,5},{13... | collective-permute-start | bytes 1179656 | tf_op jit(solution)/shard_map/ppermute | solution.py:22
  243.7 180.8 %all-reduce.13.cloned.1.call-start = ((), (), s32[]{:S(2)}) async-start(), calls=%async_computation.5 | async-start | bytes 1048576 | tf_op jit(solution)/shard_map/psum | solution.py:206
  378.7 256.0 %all-reduce.15.cloned.1.call-start = ((), (), s32[]{:S(2)}) async-start(), calls=%async_computation.7 | async-start | bytes 196608 | tf_op jit(solution)/shard_map/psum | solution.py:224
  424.5 6.4 copy-start.3
  425.7 5.2 collective-permute-start.8
  427.3 4.7 collective-permute-start.9
  484.4 9.5 %collective-permute-start.10 = (f32[64,1536]{1,0:T(8,128)S(1)}, f32[64,1536]{1,0:T(8,128)S(1)}, u32[]{:S(2)}, u32[]{:S(2)}) collective-permute-start(f32[64,1536]{1,0:T(8,128)S(1)} %get-tuple-element.20), channel_id=1, source_target_pairs={{0,4},{4,8},{8,12},{12,16},{16,20},{20,24},{24,28},{1,5},{5,9},{9,... | collective-permute-start | bytes 1179656 | tf_op jit(solution)/shard_map/ppermute | solution.py:22
  485.7 9.5 %collective-permute-start.11 = (f32[64,1536]{1,0:T(8,128)S(1)}, f32[64,1536]{1,0:T(8,128)S(1)}, u32[]{:S(2)}, u32[]{:S(2)}) collective-permute-start(f32[64,1536]{1,0:T(8,128)S(1)} %get-tuple-element.21), channel_id=1, source_target_pairs={{4,0},{8,4},{12,8},{16,12},{20,16},{24,20},{28,24},{5,1},{9,5},{13... | collective-permute-start | bytes 1179656 | tf_op jit(solution)/shard_map/ppermute | solution.py:22
  577.4 89.6 %reduce-scatter.5.cloned.1.call-start = ((), (), s32[]{:S(2)}) async-start(), calls=%async_computation.6 | async-start | bytes 294912 | tf_op jit(solution)/shard_map/reduce_scatter | solution.py:218
Sparse Core Ops, SparseCore 0:
  26.2 48.0 all-reduce.8
  229.1 57.3 all-reduce.10
  289.4 29.4 reduce-scatter.2
  378.8 45.5 all-reduce.12
  577.5 57.1 all-reduce.14
  637.5 29.4 reduce-scatter.4

commit v2 on v1

--- a/solution.py
+++ b/solution.py
@@ -181,6 +181,158 @@
     return jnp.concatenate([before, value, after], axis=1)
 
 
+def whole_sum_kernel(axis, count, value_ref, out_ref, landed, send_sem, recv_sem):
+    me = lax.axis_index(axis)
+    barrier = pltpu.get_barrier_semaphore()
+    for step in range(1, count):
+        pl.semaphore_signal(
+            barrier, inc=1, device_id={axis: lax.rem(me + step, count)},
+            device_id_type=pl.DeviceIdType.MESH,
+        )
+    pl.semaphore_wait(barrier, count - 1)
+    copies = []
+    for step in range(1, count):
+        copy = pltpu.make_async_remote_copy(
+            src_ref=value_ref,
+            dst_ref=landed.at[me],
+            send_sem=send_sem.at[step],
+            recv_sem=recv_sem.at[step],
+            device_id={axis: lax.rem(me + step, count)},
+            device_id_type=pl.DeviceIdType.MESH,
+        )
+        copy.start()
+        copies.append(copy)
+    landed[me] = value_ref[...]
+    for copy in copies:
+        copy.wait()
+    total = landed[0]
+    for slot in range(1, count):
+        total = total + landed[slot]
+    out_ref[...] = total
+
+
+def shared_sum_kernel(axis, count, value_ref, out_ref, landed, part, spread, send_sem, recv_sem):
+    me = lax.axis_index(axis)
+    chunk = value_ref.shape[0] // count
+    barrier = pltpu.get_barrier_semaphore()
+    for step in range(1, count):
+        pl.semaphore_signal(
+            barrier, inc=1, device_id={axis: lax.rem(me + step, count)},
+            device_id_type=pl.DeviceIdType.MESH,
+        )
+    pl.semaphore_wait(barrier, count - 1)
+    copies = []
+    for step in range(1, count):
+        peer = lax.rem(me + step, count)
+        copy = pltpu.make_async_remote_copy(
+            src_ref=value_ref.at[pl.ds(pl.multiple_of(peer * chunk, 8), chunk)],
+            dst_ref=landed.at[me],
+            send_sem=send_sem.at[0, step],
+            recv_sem=recv_sem.at[0, step],
+            device_id={axis: peer},
+            device_id_type=pl.DeviceIdType.MESH,
+        )
+        copy.start()
+        copies.append(copy)
+    landed[me] = value_ref[pl.ds(pl.multiple_of(me * chunk, 8), chunk), :]
+    for copy in copies:
+        copy.wait()
+    total = landed[0]
+    for slot in range(1, count):
+        total = total + landed[slot]
+    part[...] = total
+    copies = []
+    for step in range(1, count):
+        peer = lax.rem(me + step, count)
+        copy = pltpu.make_async_remote_copy(
+            src_ref=part,
+            dst_ref=spread.at[me],
+            send_sem=send_sem.at[1, step],
+            recv_sem=recv_sem.at[1, step],
+            device_id={axis: peer},
+            device_id_type=pl.DeviceIdType.MESH,
+        )
+        copy.start()
+        copies.append(copy)
+    spread[me] = part[...]
+    for copy in copies:
+        copy.wait()
+    for slot in range(count):
+        out_ref[slot * chunk : (slot + 1) * chunk, :] = spread[slot]
+
+
+def device_sum(value, axis, shared, identity):
+    count = lax.axis_size(axis)
+    rows, columns = value.shape
+    if shared:
+        chunk = rows // count
+        kernel = shared_sum_kernel
+        scratch = [
+            pltpu.VMEM((count, chunk, columns), jnp.float32),
+            pltpu.VMEM((chunk, columns), jnp.float32),
+            pltpu.VMEM((count, chunk, columns), jnp.float32),
+            pltpu.SemaphoreType.DMA((2, count)),
+            pltpu.SemaphoreType.DMA((2, count)),
+        ]
+    else:
+        kernel = whole_sum_kernel
+        scratch = [
+            pltpu.VMEM((count, rows, columns), jnp.float32),
+            pltpu.SemaphoreType.DMA((count,)),
+            pltpu.SemaphoreType.DMA((count,)),
+        ]
+    return pl.pallas_call(
+        functools.partial(kernel, axis, count),
+        out_shape=jax.ShapeDtypeStruct((rows, columns), jnp.float32),
+        in_specs=[pl.BlockSpec(memory_space=pltpu.VMEM)],
+        out_specs=pl.BlockSpec(memory_space=pltpu.VMEM),
+        scratch_shapes=scratch,
+        compiler_params=pltpu.CompilerParams(
+            collective_id=identity, has_side_effects=True, vmem_limit_bytes=24 * 1024 * 1024
+        ),
+        cost_estimate=pl.CostEstimate(
+            flops=count * rows * columns, bytes_accessed=8 * count * rows * columns, transcendentals=0
+        ),
+    )(value)
+
+
+def gram_sum(space):
+    partial = jnp.dot(space.T, space, precision=highest)
+    atoms = partial.shape[0]
+    return device_sum(jnp.pad(partial, ((0, 0), (0, -atoms % LANES))), "chan", False, 1)[:, :atoms]
+
+
+def projected_sum(space_b, signal):
+    return device_sum(
+        jnp.dot(space_b.T, signal, preferred_element_type=jnp.float32), "chan", True, 2
+    )
+
+
+def seg_sums(stats, cross, taps):
+    rows, atoms = stats.shape
+    small = jnp.concatenate([cross, taps], axis=1)
+    small = jnp.pad(small, ((0, 0), (0, -small.shape[1] % LANES)))
+    parts = small.shape[1] // LANES
+    packed = [stats[: rows // 2], stats[rows // 2 :]]
+    packed = [jnp.concatenate(packed, axis=1)] + [
+        small[:, part * LANES : (part + 1) * LANES] for part in range(parts)
+    ]
+    packed = jnp.concatenate(packed, axis=0)
+    total = packed.shape[0]
+    packed = jnp.pad(packed, ((0, -total % (8 * lax.axis_size("seg"))), (0, 0)))
+    summed = device_sum(packed, "seg", True, 3)
+    halves = summed[: rows // 2]
+    stats = jnp.concatenate([halves[:, :atoms], halves[:, atoms:]], axis=0)
+    small = jnp.concatenate(
+        [
+            summed[rows // 2 + part * atoms : rows // 2 + (part + 1) * atoms]
+            for part in range(parts)
+        ],
+        axis=1,
+    )
+    return stats, small[:, :atoms], small[:, atoms : atoms + taps.shape[1]]
+
+
 def on_device(signal, spatial, temporal, start_codes, thresholds, step_sizes, breaks):
     chan_rows, seg_len = signal.shape
     atoms_all, tap_count = temporal.shape
@@ -192,18 +344,17 @@
     )
     allowed = jnp.where(jnp.any(crosses, axis=0) | ~inside, 0.0, 1.0).astype(jnp.float32)
     inside = inside.astype(jnp.float32)
-    raw_start = lax.psum(jnp.dot(spatial.T, spatial, precision=highest), "chan")
+    raw_start = gram_sum(spatial)
     scaling = 1.0 / jnp.sqrt(jnp.diag(raw_start) + epsilon)
     space_loc = spatial * scaling[None, :]
     gram_matrix = raw_start * scaling[:, None] * scaling[None, :]
     kernel = temporal / jnp.sqrt(jnp.sum(temporal * temporal, axis=1, keepdims=True) + epsilon)
     latent = start_codes
     limits = step_sizes * thresholds
-    rows_share = chan_rows // lax.axis_size("seg")
     for sweep_index in range(OUTER):
         space_b = space_loc.astype(jnp.bfloat16)
         kernel_b = kernel.astype(jnp.bfloat16)
-        projected = lax.psum(jnp.dot(space_b.T, signal, preferred_element_type=jnp.float32), "chan")
+        projected = projected_sum(space_b, signal)
         wide = widened(projected)
         (latent,) = run_steps(
             ITERS // 2, False, widened(latent), wide, kernel_b, gram_matrix,
@@ -215,29 +366,18 @@
         )
         taps_part = lags[:, 1 : tap_count + 1][:, ::-1]
         rebuilt_b = rebuilt.astype(jnp.bfloat16)
-        stats_rows = lax.psum_scatter(
+        stats, cross_gram, raw_kernel = seg_sums(
             jnp.dot(signal, rebuilt_b.T, preferred_element_type=jnp.float32),
-            "seg",
-            scatter_dimension=0,
-            tiled=True,
-        )
-        summed = lax.psum(
-            jnp.concatenate(
-                [jnp.dot(rebuilt, rebuilt.T, precision=highest), taps_part], axis=1
-            ),
-            "seg",
-        )
-        cross_gram, raw_kernel = summed[:, :atoms_all], summed[:, atoms_all:]
-        seg_first = lax.axis_index("seg") * rows_share
-        own_space = lax.dynamic_slice_in_dim(space_loc, seg_first, rows_share, 0)
-        raw_rows = stats_rows - jnp.dot(
-            own_space, cross_gram - jnp.diag(jnp.diag(cross_gram)), precision=highest
-        )
-        squares = lax.psum(jnp.sum(raw_rows * raw_rows, axis=0), ("seg", "chan"))
-        new_rows = raw_rows / jnp.sqrt(squares + epsilon)[None, :]
-        space_loc = lax.all_gather(new_rows, "seg", axis=0, tiled=True)
-        if sweep_index + 1 < OUTER:
-            gram_matrix = lax.psum(jnp.dot(space_loc.T, space_loc, precision=highest), "chan")
+            jnp.dot(rebuilt, rebuilt.T, precision=highest),
+            taps_part,
+        )
+        raw_space = stats - jnp.dot(
+            space_loc, cross_gram - jnp.diag(jnp.diag(cross_gram)), precision=highest
+        )
+        raw_gram = gram_sum(raw_space)
+        scaling = 1.0 / jnp.sqrt(jnp.diag(raw_gram) + epsilon)
+        space_loc = raw_space * scaling[None, :]
+        gram_matrix = raw_gram * scaling[:, None] * scaling[None, :]
         kernel = raw_kernel / jnp.sqrt(
             jnp.sum(raw_kernel * raw_kernel, axis=1, keepdims=True) + epsilon
         )

time: 734 us -> 441 us (0.60)
  waiting for transfers between devices: 225 us -> 3.63 us
  blocking collectives: 135 us -> 0 us
  Pallas kernels: 265 us -> 362 us
  between operations: 14.7 us -> 1.4 us
    psum x4 -> x0, waiting for transfers between devices: 164 us -> none  [the longest x2 95.7 us: on_device(): lax.psum(jnp.concatenate([jnp.dot(rebuilt, rebuilt.T, precision=highest),...]
    psum x4 -> x0, blocking collectives: 102 us -> none  [the longest x2 77.1 us: on_device(): squares = lax.psum(jnp.sum(raw_rows * raw_rows, axis=0), ('seg', 'chan'))]
    pallas_call x0 -> x7, Pallas kernels: none -> 96.4 us  [device_sum(): pl.pallas_call(functools.partial(kernel, axis, count), out_shape=jax.Shap...]
    reduce_scatter x2 -> x0, waiting for transfers between devices: 56.4 us -> none  [on_device(): lax.psum_scatter(jnp.dot(signal, rebuilt_b.T, preferred_element_type=jnp....]
    all_gather x2 -> x0, blocking collectives: 32.3 us -> none  [on_device(): space_loc = lax.all_gather(new_rows, 'seg', axis=0, tiled=True)]
  transfers between devices with their start and end apart: 18 -> 12, of which waited for: 10 -> 3; matrix products, arithmetic and copies ran while one was open for 4% -> 1% of each run, Pallas kernels for 0% -> 0%
where the time goes in v2:
time: 441 us
  Pallas kernels  362 us (82%)
  starting transfers between devices  41.6 us (9%)
  matrix products  15 us (3%)
  local copies, waits for them, and re-layouts  13.5 us (3%)
    pallas_call x4, Pallas kernels, run_steps(): pl.pallas_call(functools.partial(steps_kernel, steps, last, atoms, blocks...  266 us
    pallas_call x7, Pallas kernels, device_sum(): pl.pallas_call(functools.partial(kernel, axis, count), out_shape=jax.Shap...  96.4 us
    ppermute x12, starting transfers between devices, passed_along(): lax.ppermute(value, axis, [(source, source + steps) for source in range(l...  41.6 us
  transfers between devices with their start and end apart: 12, of which 3 were waited for; matrix products, arithmetic and copies ran while one was open for 1% of the time, Pallas kernels for 0%

profile of v2, /device:TPU:25, one launch (start us, length us, event | category | flops | bytes accessed | tf_op | source)
XLA Modules:
  0.0 440.8 jit_solution(6977570712508093579)
XLA Ops:
  0.6 1.4 fusion.45
  2.1 4.2 shard_map.94
  7.2 3.1 fusion.7.value_ref
  10.3 13.7 %shard_map.95 = f32[64,2048]{1,0:T(8,128)S(1)} custom-call(f32[64,2048]{1,0:T(8,128)S(1)} %fusion.7.value_ref), custom_call_target="tpu_custom_call" | custom-call | flops 524288 | bytes 4194304 | tf_op jit(solution)/shard_map/pallas_call | solution.py:284
  24.9 1.3 collective-permute-start.2
  26.2 5.4 %collective-permute-start.3 = (f32[64,1536]{1,0:T(8,128)}, f32[64,1536]{1,0:T(8,128)S(1)}, u32[]{:S(2)}, u32[]{:S(2)}) collective-permute-start(f32[64,1536]{1,0:T(8,128)} %get-tuple-element.43), channel_id=1, source_target_pairs={{4,0},{8,4},{12,8},{16,12},{20,16},{24,20},{28,24},{5,1},{9,5},{13... | collective-permute-start | bytes 1179656 | tf_op jit(solution)/shard_map/ppermute | solution.py:22
  32.6 1.3 collective-permute-start
  33.9 4.3 collective-permute-start.1
  40.2 52.3 %shard_map.96 = f32[64,2048]{1,0:T(8,128)S(1)} custom-call(f32[64]{0:T(128)S(1)} %copy-done, f32[64]{0:T(128)S(1)} %mul.71.limit_ref, f32[64,5120]{1,0:T(8,128)S(1)} %pad_maximum_fusion.latent_in, f32[64,5120]{1,0:T(8,128)S(1)} %pad_maximum_fusion.1.proj_in, f32[64,512]{1,0:T(8,128)S(1)} %pad.36.taps_ref, f32[64,512]{1,0:T(8,128)S(1)} %pad.37.flipped_ref, ...), custom_call_target="tpu_custom_call" | custom-call | flops 2516582400 | bytes 2621440 | tf_op jit(solution)/shard_map/pallas_call | solution.py:160
  92.6 1.3 collective-permute-start.4
  93.9 7.8 %collective-permute-start.5 = (f32[64,1536]{1,0:T(8,128)S(1)}, f32[64,1536]{1,0:T(8,128)S(1)}, u32[]{:S(2)}, u32[]{:S(2)}) collective-permute-start(f32[64,1536]{1,0:T(8,128)S(1)} %get-tuple-element.41), channel_id=1, source_target_pairs={{4,0},{8,4},{12,8},{16,12},{20,16},{24,20},{28,24},{5,1},{9,5},{13... | collective-permute-start | bytes 1179656 | tf_op jit(solution)/shard_map/ppermute | solution.py:22
  101.8 1.3 collective-permute-done.5
  103.2 80.5 %shard_map.97 = (f32[64,2048]{1,0:T(8,128)S(1)}, f32[64,2048]{1,0:T(8,128)S(1)}, f32[64,384]{1,0:T(8,128)S(1)}) custom-call(f32[64]{0:T(128)S(1)} %copy-done, f32[64]{0:T(128)S(1)} %mul.71.limit_ref, f32[64,5120]{1,0:T(8,128)S(1)} %pad_maximum_fusion.2.latent_in, f32[64,5120]{1,0:T(8,128)S(1)} %pad_maximum_fusion.1.proj_in, f32[64,512]{1,0:T(8,128)S(1)} %pad.36.taps_ref, ...), custom_call_target="tpu_custom_call" | custom-call | flops 2516582400 | bytes 2621440 | tf_op jit(solution)/shard_map/pallas_call | solution.py:160
  184.3 1.2 convolution_bitcast_fusion.1
  186.3 26.4 %shard_map.98 = f32[704,128]{1,0:T(8,128)S(1)} custom-call(f32[704,128]{1,0:T(8,128)S(1)} %pad_maximum_fusion.6.value_ref), custom_call_target="tpu_custom_call" | custom-call | flops 720896 | bytes 5767168 | tf_op jit(solution)/shard_map/pallas_call | solution.py:284
  213.7 1.1 convolution_subtract_fusion
  215.9 5.8 %shard_map.99 = f32[64,128]{1,0:T(8,128)S(1)} custom-call(f32[64,128]{1,0:T(8,128)S(1)} %pad.39.value_ref), custom_call_target="tpu_custom_call" | custom-call | flops 32768 | bytes 262144 | tf_op jit(solution)/shard_map/pallas_call | solution.py:284
  222.6 3.1 fusion.1.value_ref
  226.0 14.3 %shard_map.100 = f32[64,2048]{1,0:T(8,128)S(1)} custom-call(f32[64,2048]{1,0:T(8,128)S(1)} %fusion.1.value_ref), custom_call_target="tpu_custom_call" | custom-call | flops 524288 | bytes 4194304 | tf_op jit(solution)/shard_map/pallas_call | solution.py:284
  241.2 1.3 collective-permute-start.8
  242.4 3.9 collective-permute-start.9
  249.9 1.3 collective-permute-start.6
  251.2 4.3 collective-permute-start.7
  256.8 52.3 %shard_map.101 = f32[64,2048]{1,0:T(8,128)S(1)} custom-call(f32[64]{0:T(128)S(1)} %copy-done, f32[64]{0:T(128)S(1)} %mul.71.limit_ref, f32[64,5120]{1,0:T(8,128)S(1)} %pad_maximum_fusion.3.latent_in, f32[64,5120]{1,0:T(8,128)S(1)} %pad_maximum_fusion.4.proj_in, f32[64,512]{1,0:T(8,128)S(1)} %pad.40.taps_ref, f32[64,512]{1,0:T(8,128)S(1)} %pad.41.flipped_ref, ...), custom_call_target="tpu_custom_call" | custom-call | flops 2516582400 | bytes 2621440 | tf_op jit(solution)/shard_map/pallas_call | solution.py:160
  309.2 1.3 collective-permute-start.10
  310.5 8.2 %collective-permute-start.11 = (f32[64,1536]{1,0:T(8,128)S(1)}, f32[64,1536]{1,0:T(8,128)S(1)}, u32[]{:S(2)}, u32[]{:S(2)}) collective-permute-start(f32[64,1536]{1,0:T(8,128)S(1)} %get-tuple-element.33), channel_id=1, source_target_pairs={{4,0},{8,4},{12,8},{16,12},{20,16},{24,20},{28,24},{5,1},{9,5},{13... | collective-permute-start | bytes 1179656 | tf_op jit(solution)/shard_map/ppermute | solution.py:22
  318.8 1.3 collective-permute-done.11
  320.2 80.6 %shard_map.102 = (f32[64,2048]{1,0:T(8,128)}, f32[64,2048]{1,0:T(8,128)S(1)}, f32[64,384]{1,0:T(8,128)S(1)}) custom-call(f32[64]{0:T(128)S(1)} %copy-done, f32[64]{0:T(128)S(1)} %mul.71.limit_ref, f32[64,5120]{1,0:T(8,128)S(1)} %pad_maximum_fusion.5.latent_in, f32[64,5120]{1,0:T(8,128)S(1)} %pad_maximum_fusion.4.proj_in, f32[64,512]{1,0:T(8,128)S(1)} %pad.40.taps_ref, ...), custom_call_target="tpu_custom_call" | custom-call | flops 2516582400 | bytes 2621440 | tf_op jit(solution)/shard_map/pallas_call | solution.py:160
  401.4 1.2 convolution_bitcast_fusion
  403.4 26.5 %shard_map.103 = f32[704,128]{1,0:T(8,128)S(1)} custom-call(f32[704,128]{1,0:T(8,128)S(1)} %pad_maximum_fusion.7.value_ref), custom_call_target="tpu_custom_call" | custom-call | flops 720896 | bytes 5767168 | tf_op jit(solution)/shard_map/pallas_call | solution.py:284
  431.7 1.0 fusion.49
  433.5 5.5 %shard_map.104 = f32[64,128]{1,0:T(8,128)S(1)} custom-call(f32[64,128]{1,0:T(8,128)S(1)} %pad.43.value_ref), custom_call_target="tpu_custom_call" | custom-call | flops 32768 | bytes 262144 | tf_op jit(solution)/shard_map/pallas_call | solution.py:284
  (109 shorter events, 20.8 us)
Async XLA Ops:
  0.6 6.5 %copy-start.3 = (f32[1024,64]{0,1:T(8,128)S(1)}, f32[1024,64]{0,1:T(8,128)}, u32[]{:S(2)}) copy-start(f32[1024,64]{0,1:T(8,128)} %param.8) | copy-start | bytes 786436
  10.3 21.4 %copy-start.4 = (f32[64,2048]{1,0:T(8,128)S(1)}, f32[64,2048]{1,0:T(8,128)}, u32[]{:S(2)}) copy-start(f32[64,2048]{1,0:T(8,128)} %param.10) | copy-start | bytes 1572868
  23.9 14.3 %copy-start.5 = (f32[64,256]{1,0:T(8,128)S(1)}, f32[64,256]{1,0:T(8,128)}, u32[]{:S(2)}) copy-start(f32[64,256]{1,0:T(8,128)} %param.9) | copy-start | bytes 196612
  24.9 15.1 %collective-permute-start.2 = (f32[64,1536]{1,0:T(8,128)}, f32[64,1536]{1,0:T(8,128)S(1)}, u32[]{:S(2)}, u32[]{:S(2)}) collective-permute-start(f32[64,1536]{1,0:T(8,128)} %get-tuple-element.42), channel_id=1, source_target_pairs={{0,4},{4,8},{8,12},{12,16},{16,20},{20,24},{24,28},{1,5},{5,9},{9,... | collective-permute-start | bytes 1179656 | tf_op jit(solution)/shard_map/ppermute | solution.py:22
  26.2 13.6 %copy-start = (f32[64]{0:T(128)S(1)}, f32[64]{0:T(128)}, u32[]{:S(2)}) copy-start(f32[64]{0:T(128)} %step_ref.7) | copy-start | bytes 772
  26.2 13.6 %copy-start.7 = (f32[64]{0:T(128)S(1)}, f32[64]{0:T(128)}, u32[]{:S(2)}) copy-start(f32[64]{0:T(128)} %param.11) | copy-start | bytes 772
  26.2 13.6 %copy-start.6 = (s32[16]{0:T(128)S(1)}, s32[16]{0:T(128)}, u32[]{:S(2)}) copy-start(s32[16]{0:T(128)} %param.13) | copy-start | bytes 196
  26.2 13.8 %collective-permute-start.3 = (f32[64,1536]{1,0:T(8,128)}, f32[64,1536]{1,0:T(8,128)S(1)}, u32[]{:S(2)}, u32[]{:S(2)}) collective-permute-start(f32[64,1536]{1,0:T(8,128)} %get-tuple-element.43), channel_id=1, source_target_pairs={{4,0},{8,4},{12,8},{16,12},{20,16},{24,20},{28,24},{5,1},{9,5},{13... | collective-permute-start | bytes 1179656 | tf_op jit(solution)/shard_map/ppermute | solution.py:22
  32.6 7.6 %collective-permute-start = (f32[64,1536]{1,0:T(8,128)}, f32[64,1536]{1,0:T(8,128)S(1)}, u32[]{:S(2)}, u32[]{:S(2)}) collective-permute-start(f32[64,1536]{1,0:T(8,128)} %get-tuple-element.44), channel_id=1, source_target_pairs={{0,4},{4,8},{8,12},{12,16},{16,20},{20,24},{24,28},{1,5},{5,9},{9,... | collective-permute-start | bytes 1179656 | tf_op jit(solution)/shard_map/ppermute | solution.py:22
  33.9 6.3 %collective-permute-start.1 = (f32[64,1536]{1,0:T(8,128)}, f32[64,1536]{1,0:T(8,128)S(1)}, u32[]{:S(2)}, u32[]{:S(2)}) collective-permute-start(f32[64,1536]{1,0:T(8,128)} %get-tuple-element.45), channel_id=1, source_target_pairs={{4,0},{8,4},{12,8},{16,12},{20,16},{24,20},{28,24},{5,1},{9,5},{13... | collective-permute-start | bytes 1179656 | tf_op jit(solution)/shard_map/ppermute | solution.py:22
  92.6 9.2 %collective-permute-start.4 = (f32[64,1536]{1,0:T(8,128)S(1)}, f32[64,1536]{1,0:T(8,128)S(1)}, u32[]{:S(2)}, u32[]{:S(2)}) collective-permute-start(f32[64,1536]{1,0:T(8,128)S(1)} %get-tuple-element.40), channel_id=1, source_target_pairs={{0,4},{4,8},{8,12},{12,16},{16,20},{20,24},{24,28},{1,5},{5,9},{9,... | collective-permute-start | bytes 1179656 | tf_op jit(solution)/shard_map/ppermute | solution.py:22
  93.9 9.2 %collective-permute-start.5 = (f32[64,1536]{1,0:T(8,128)S(1)}, f32[64,1536]{1,0:T(8,128)S(1)}, u32[]{:S(2)}, u32[]{:S(2)}) collective-permute-start(f32[64,1536]{1,0:T(8,128)S(1)} %get-tuple-element.41), channel_id=1, source_target_pairs={{4,0},{8,4},{12,8},{16,12},{20,16},{24,20},{28,24},{5,1},{9,5},{13... | collective-permute-start | bytes 1179656 | tf_op jit(solution)/shard_map/ppermute | solution.py:22
  103.2 81.1 %copy-start.1 = (bf16[1024,2048]{1,0:T(8,128)(2,1)S(1)}, bf16[1024,2048]{1,0:T(8,128)(2,1)}, u32[]{:S(2)}) copy-start(bf16[1024,2048]{1,0:T(8,128)(2,1)} %param.7) | copy-start | bytes 12582916
  241.2 14.4 %collective-permute-start.8 = (f32[64,1536]{1,0:T(8,128)}, f32[64,1536]{1,0:T(8,128)S(1)}, u32[]{:S(2)}, u32[]{:S(2)}) collective-permute-start(f32[64,1536]{1,0:T(8,128)} %get-tuple-element.34), channel_id=1, source_target_pairs={{0,4},{4,8},{8,12},{12,16},{16,20},{20,24},{24,28},{1,5},{5,9},{9,... | collective-permute-start | bytes 1179656 | tf_op jit(solution)/shard_map/ppermute | solution.py:22
  242.4 13.2 %collective-permute-start.9 = (f32[64,1536]{1,0:T(8,128)S(1)}, f32[64,1536]{1,0:T(8,128)S(1)}, u32[]{:S(2)}, u32[]{:S(2)}) collective-permute-start(f32[64,1536]{1,0:T(8,128)S(1)} %get-tuple-element.35), channel_id=1, source_target_pairs={{4,0},{8,4},{12,8},{16,12},{20,16},{24,20},{28,24},{5,1},{9,5},{13... | collective-permute-start | bytes 1179656 | tf_op jit(solution)/shard_map/ppermute | solution.py:22
  249.9 5.8 %collective-permute-start.6 = (f32[64,1536]{1,0:T(8,128)}, f32[64,1536]{1,0:T(8,128)S(1)}, u32[]{:S(2)}, u32[]{:S(2)}) collective-permute-start(f32[64,1536]{1,0:T(8,128)} %get-tuple-element.38), channel_id=1, source_target_pairs={{0,4},{4,8},{8,12},{12,16},{16,20},{20,24},{24,28},{1,5},{5,9},{9,... | collective-permute-start | bytes 1179656 | tf_op jit(solution)/shard_map/ppermute | solution.py:22
  251.2 5.6 %collective-permute-start.7 = (f32[64,1536]{1,0:T(8,128)S(1)}, f32[64,1536]{1,0:T(8,128)S(1)}, u32[]{:S(2)}, u32[]{:S(2)}) collective-permute-start(f32[64,1536]{1,0:T(8,128)S(1)} %get-tuple-element.39), channel_id=1, source_target_pairs={{4,0},{8,4},{12,8},{16,12},{20,16},{24,20},{28,24},{5,1},{9,5},{13... | collective-permute-start | bytes 1179656 | tf_op jit(solution)/shard_map/ppermute | solution.py:22
  309.2 9.5 %collective-permute-start.10 = (f32[64,1536]{1,0:T(8,128)S(1)}, f32[64,1536]{1,0:T(8,128)S(1)}, u32[]{:S(2)}, u32[]{:S(2)}) collective-permute-start(f32[64,1536]{1,0:T(8,128)S(1)} %get-tuple-element.32), channel_id=1, source_target_pairs={{0,4},{4,8},{8,12},{12,16},{16,20},{20,24},{24,28},{1,5},{5,9},{9,... | collective-permute-start | bytes 1179656 | tf_op jit(solution)/shard_map/ppermute | solution.py:22
  310.5 9.5 %collective-permute-start.11 = (f32[64,1536]{1,0:T(8,128)S(1)}, f32[64,1536]{1,0:T(8,128)S(1)}, u32[]{:S(2)}, u32[]{:S(2)}) collective-permute-start(f32[64,1536]{1,0:T(8,128)S(1)} %get-tuple-element.33), channel_id=1, source_target_pairs={{4,0},{8,4},{12,8},{16,12},{20,16},{24,20},{28,24},{5,1},{9,5},{13... | collective-permute-start | bytes 1179656 | tf_op jit(solution)/shard_map/ppermute | solution.py:22
  320.2 81.2 %copy-start.2 = (bf16[1024,2048]{1,0:T(8,128)(2,1)S(1)}, bf16[1024,2048]{1,0:T(8,128)(2,1)}, u32[]{:S(2)}) copy-start(bf16[1024,2048]{1,0:T(8,128)(2,1)} %param.7) | copy-start | bytes 12582916

commit v3 on v2

--- a/solution.py
+++ b/solution.py
@@ -35,9 +35,9 @@
     *rest,
 ):
     if last:
-        latent_out, rebuilt_out, lags_out, latent, proj, mixed, forward, backward = rest
+        latent_out, rebuilt_out, lags_out, latent, proj, mixed, forward, backward, stage = rest
     else:
-        latent_out, latent, proj, mixed, forward, backward = rest
+        latent_out, latent, proj, mixed, forward, backward, _ = rest
 
     def spread(block, carry):
         rows = pl.ds(pl.multiple_of(block * atoms, atoms), atoms)
@@ -46,7 +46,7 @@
         proj[rows, :] = proj_in[:, columns]
         return carry
 
-    lax.fori_loop(0, blocks, spread, 0)
+    lax.fori_loop(0, blocks, spread, 0, unroll=4)
 
     def build(atom, carry):
         for source, target in ((taps_ref, forward), (flipped_ref, backward)):
@@ -58,7 +58,7 @@
                 ]
         return carry
 
-    lax.fori_loop(0, atoms, build, 0)
+    lax.fori_loop(0, atoms, build, 0, unroll=4)
 
     def rows_of(atom):
         return pl.ds(atom, blocks, stride=atoms)
@@ -74,14 +74,19 @@
         )
         return carry
 
-    def mix(block, carry, matrix_ref):
-        rows = pl.ds(pl.multiple_of(block * atoms, atoms), atoms)
-        rebuilt = mixed[rows, :]
+    def mix(pair, carry, matrix_ref):
+        rows = pl.ds(pl.multiple_of(pair * 2 * atoms, 2 * atoms), 2 * atoms)
+        both = mixed[rows, :]
+        rebuilt = jnp.concatenate([both[:atoms], both[atoms:]], axis=1)
         high = rebuilt.astype(jnp.bfloat16)
         low = (rebuilt - high.astype(jnp.float32)).astype(jnp.bfloat16)
-        stacked = jnp.concatenate([high, low, high], axis=0)
-        mixed[rows, :] = proj[rows, :] - jnp.dot(
-            matrix_ref[...], stacked, preferred_element_type=jnp.float32
+        blended = jnp.dot(
+            matrix_ref[...],
+            jnp.concatenate([high, low, high], axis=0),
+            preferred_element_type=jnp.float32,
+        )
+        mixed[rows, :] = proj[rows, :] - jnp.concatenate(
+            [blended[:, :LANES], blended[:, LANES:]], axis=0
         )
         return carry
 
@@ -103,7 +108,7 @@
 
     def one_step(iteration, carry):
         lax.fori_loop(0, atoms, convolve, 0, unroll=8)
-        lax.fori_loop(0, blocks, functools.partial(mix, matrix_ref=gram_ref), 0, unroll=4)
+        lax.fori_loop(0, blocks // 2, functools.partial(mix, matrix_ref=gram_ref), 0, unroll=4)
         lax.fori_loop(0, atoms, shrink, 0, unroll=8)
         return carry
 
@@ -117,7 +122,9 @@
     for block in range(own):
         first = (HALO + block) * atoms
         rebuilt_out[:, block * LANES : (block + 1) * LANES] = mixed[first : first + atoms, :]
-    lax.fori_loop(HALO, HALO + own, functools.partial(mix, matrix_ref=plain_ref), 0, unroll=4)
+    lax.fori_loop(
+        HALO // 2, (HALO + own) // 2, functools.partial(mix, matrix_ref=plain_ref), 0, unroll=4
+    )
 
     def lagged(atom, carry):
         codes = latent[rows_of(atom), :]
@@ -133,13 +140,17 @@
             pair, twice, (((0,), (0,)), ((), ())), preferred_element_type=jnp.float32
         )
         half = LANES // 2
-        while half >= 1:
+        while half >= 8:
             total = total[:half] + pltpu.roll(total[half:], 3 * LANES - half, 1)
             half //= 2
-        lags_out[pl.ds(atom, 1), :] = total
-        return carry
-
-    lax.fori_loop(0, atoms, lagged, 0, unroll=2)
+        stage[atom] = total
+        return carry
+
+    lax.fori_loop(0, atoms, lagged, 0, unroll=8)
+    total = stage[:, 0, :]
+    for row in range(1, 8):
+        total = total + pltpu.roll(stage[:, row, :], 3 * LANES - row, 1)
+    lags_out[...] = total
 
 
 def run_steps(steps, last, latent, projected, kernel_b, gram_matrix, step, limit, allowed, inside):
@@ -163,7 +174,8 @@
         in_specs=[in_smem] * 2 + [in_vmem] * 8,
         out_specs=[in_vmem] * len(out),
         scratch_shapes=[pltpu.VMEM((blocks * atoms, LANES), jnp.float32)] * 3
-        + [pltpu.VMEM((atoms, 3 * LANES, LANES), jnp.bfloat16)] * 2,
+        + [pltpu.VMEM((atoms, 3 * LANES, LANES), jnp.bfloat16)] * 2
+        + [pltpu.VMEM((atoms, 8, 3 * LANES), jnp.float32)],
         compiler_params=pltpu.CompilerParams(vmem_limit_bytes=48 * 1024 * 1024),
         cost_estimate=pl.CostEstimate(
             flops=4 * steps * atoms * width * 3 * LANES, bytes_accessed=8 * atoms * width, transcendentals=0

time: 441 us -> 371 us (0.84)
  Pallas kernels: 362 us -> 292 us
    pallas_call x4, Pallas kernels: 266 us -> 195 us  [run_steps(): pl.pallas_call(functools.partial(steps_kernel, steps, last, atoms, blocks...]
  transfers between devices with their start and end apart: 12 -> 12, of which waited for: 3 -> 3; matrix products, arithmetic and copies ran while one was open for 1% -> 2% of each run, Pallas kernels for 0% -> 0%
where the time goes in v3:
time: 371 us; the launch traced here: 370 us
  Pallas kernels  292 us (79%)
  starting transfers between devices  41.9 us (11%)
  matrix products  15 us (4%)
  local copies, waits for them, and re-layouts  13.5 us (4%)
    pallas_call x4, Pallas kernels, run_steps(): pl.pallas_call(functools.partial(steps_kernel, steps, last, atoms, blocks...  195 us
    pallas_call x7, Pallas kernels, device_sum(): pl.pallas_call(functools.partial(kernel, axis, count), out_shape=jax.Shap...  96.4 us
    ppermute x12, starting transfers between devices, passed_along(): lax.ppermute(value, axis, [(source, source + steps) for source in range(l...  41.9 us
  transfers between devices with their start and end apart: 12, of which 3 were waited for; matrix products, arithmetic and copies ran while one was open for 2% of the time, Pallas kernels for 0%

profile of v3, /device:TPU:25, one launch (start us, length us, event | category | flops | bytes accessed | tf_op | source)
XLA Modules:
  0.0 370.3 jit_solution(10294853544762817712)
XLA Ops:
  0.6 1.4 fusion.45
  2.1 4.2 %shard_map.94 = f32[64,128]{1,0:T(8,128)S(1)} custom-call(f32[64,128]{1,0:T(8,128)S(1)} %pad.35.value_ref), custom_call_target="tpu_custom_call" | custom-call | flops 32768 | bytes 262144 | tf_op jit(solution)/shard_map/pallas_call | solution.py:296
  7.2 3.1 fusion.7.value_ref
  10.3 13.7 %shard_map.95 = f32[64,2048]{1,0:T(8,128)S(1)} custom-call(f32[64,2048]{1,0:T(8,128)S(1)} %fusion.7.value_ref), custom_call_target="tpu_custom_call" | custom-call | flops 524288 | bytes 4194304 | tf_op jit(solution)/shard_map/pallas_call | solution.py:296
  24.9 1.3 collective-permute-start.2
  26.2 5.4 %collective-permute-start.3 = (f32[64,1536]{1,0:T(8,128)}, f32[64,1536]{1,0:T(8,128)S(1)}, u32[]{:S(2)}, u32[]{:S(2)}) collective-permute-start(f32[64,1536]{1,0:T(8,128)} %get-tuple-element.43), channel_id=1, source_target_pairs={{4,0},{8,4},{12,8},{16,12},{20,16},{24,20},{28,24},{5,1},{9,5},{13... | collective-permute-start | bytes 1179656 | tf_op jit(solution)/shard_map/ppermute | solution.py:22
  32.6 1.3 collective-permute-start
  33.9 4.3 %collective-permute-start.1 = (f32[64,1536]{1,0:T(8,128)}, f32[64,1536]{1,0:T(8,128)S(1)}, u32[]{:S(2)}, u32[]{:S(2)}) collective-permute-start(f32[64,1536]{1,0:T(8,128)} %get-tuple-element.45), channel_id=1, source_target_pairs={{4,0},{8,4},{12,8},{16,12},{20,16},{24,20},{28,24},{5,1},{9,5},{13... | collective-permute-start | bytes 1179656 | tf_op jit(solution)/shard_map/ppermute | solution.py:22
  40.2 43.9 %shard_map.96 = f32[64,2048]{1,0:T(8,128)S(1)} custom-call(f32[64]{0:T(128)S(1)} %copy-done, f32[64]{0:T(128)S(1)} %mul.71.limit_ref, f32[64,5120]{1,0:T(8,128)S(1)} %pad_maximum_fusion.latent_in, f32[64,5120]{1,0:T(8,128)S(1)} %pad_maximum_fusion.1.proj_in, f32[64,512]{1,0:T(8,128)S(1)} %pad.36.taps_ref, f32[64,512]{1,0:T(8,128)S(1)} %pad.37.flipped_ref, ...), custom_call_target="tpu_custom_call" | custom-call | flops 2516582400 | bytes 2621440 | tf_op jit(solution)/shard_map/pallas_call | solution.py:171
  84.2 1.3 collective-permute-start.4
  85.5 8.0 %collective-permute-start.5 = (f32[64,1536]{1,0:T(8,128)S(1)}, f32[64,1536]{1,0:T(8,128)S(1)}, u32[]{:S(2)}, u32[]{:S(2)}) collective-permute-start(f32[64,1536]{1,0:T(8,128)S(1)} %get-tuple-element.41), channel_id=1, source_target_pairs={{4,0},{8,4},{12,8},{16,12},{20,16},{24,20},{28,24},{5,1},{9,5},{13... | collective-permute-start | bytes 1179656 | tf_op jit(solution)/shard_map/ppermute | solution.py:22
  93.6 1.1 collective-permute-done.5
  94.8 53.8 %shard_map.97 = (f32[64,2048]{1,0:T(8,128)S(1)}, f32[64,2048]{1,0:T(8,128)S(1)}, f32[64,384]{1,0:T(8,128)S(1)}) custom-call(f32[64]{0:T(128)S(1)} %copy-done, f32[64]{0:T(128)S(1)} %mul.71.limit_ref, f32[64,5120]{1,0:T(8,128)S(1)} %pad_maximum_fusion.2.latent_in, f32[64,5120]{1,0:T(8,128)S(1)} %pad_maximum_fusion.1.proj_in, f32[64,512]{1,0:T(8,128)S(1)} %pad.36.taps_ref, ...), custom_call_target="tpu_custom_call" | custom-call | flops 2516582400 | bytes 2621440 | tf_op jit(solution)/shard_map/pallas_call | solution.py:171
  149.2 1.2 convolution_bitcast_fusion.1
  151.2 26.4 %shard_map.98 = f32[704,128]{1,0:T(8,128)S(1)} custom-call(f32[704,128]{1,0:T(8,128)S(1)} %pad_maximum_fusion.6.value_ref), custom_call_target="tpu_custom_call" | custom-call | flops 720896 | bytes 5767168 | tf_op jit(solution)/shard_map/pallas_call | solution.py:296
  178.6 1.1 convolution_subtract_fusion
  180.7 5.8 %shard_map.99 = f32[64,128]{1,0:T(8,128)S(1)} custom-call(f32[64,128]{1,0:T(8,128)S(1)} %pad.39.value_ref), custom_call_target="tpu_custom_call" | custom-call | flops 32768 | bytes 262144 | tf_op jit(solution)/shard_map/pallas_call | solution.py:296
  187.5 3.1 fusion.1.value_ref
  190.9 14.3 %shard_map.100 = f32[64,2048]{1,0:T(8,128)S(1)} custom-call(f32[64,2048]{1,0:T(8,128)S(1)} %fusion.1.value_ref), custom_call_target="tpu_custom_call" | custom-call | flops 524288 | bytes 4194304 | tf_op jit(solution)/shard_map/pallas_call | solution.py:296
  206.0 1.3 collective-permute-start.8
  207.3 3.8 %collective-permute-start.9 = (f32[64,1536]{1,0:T(8,128)S(1)}, f32[64,1536]{1,0:T(8,128)S(1)}, u32[]{:S(2)}, u32[]{:S(2)}) collective-permute-start(f32[64,1536]{1,0:T(8,128)S(1)} %get-tuple-element.35), channel_id=1, source_target_pairs={{4,0},{8,4},{12,8},{16,12},{20,16},{24,20},{28,24},{5,1},{9,5},{13... | collective-permute-start | bytes 1179656 | tf_op jit(solution)/shard_map/ppermute | solution.py:22
  214.6 1.3 collective-permute-start.6
  215.9 4.3 %collective-permute-start.7 = (f32[64,1536]{1,0:T(8,128)S(1)}, f32[64,1536]{1,0:T(8,128)S(1)}, u32[]{:S(2)}, u32[]{:S(2)}) collective-permute-start(f32[64,1536]{1,0:T(8,128)S(1)} %get-tuple-element.39), channel_id=1, source_target_pairs={{4,0},{8,4},{12,8},{16,12},{20,16},{24,20},{28,24},{5,1},{9,5},{13... | collective-permute-start | bytes 1179656 | tf_op jit(solution)/shard_map/ppermute | solution.py:22
  221.5 43.9 %shard_map.101 = f32[64,2048]{1,0:T(8,128)S(1)} custom-call(f32[64]{0:T(128)S(1)} %copy-done, f32[64]{0:T(128)S(1)} %mul.71.limit_ref, f32[64,5120]{1,0:T(8,128)S(1)} %pad_maximum_fusion.3.latent_in, f32[64,5120]{1,0:T(8,128)S(1)} %pad_maximum_fusion.4.proj_in, f32[64,512]{1,0:T(8,128)S(1)} %pad.40.taps_ref, f32[64,512]{1,0:T(8,128)S(1)} %pad.41.flipped_ref, ...), custom_call_target="tpu_custom_call" | custom-call | flops 2516582400 | bytes 2621440 | tf_op jit(solution)/shard_map/pallas_call | solution.py:171
  265.5 1.3 collective-permute-start.10
  266.8 8.5 %collective-permute-start.11 = (f32[64,1536]{1,0:T(8,128)S(1)}, f32[64,1536]{1,0:T(8,128)S(1)}, u32[]{:S(2)}, u32[]{:S(2)}) collective-permute-start(f32[64,1536]{1,0:T(8,128)S(1)} %get-tuple-element.33), channel_id=1, source_target_pairs={{4,0},{8,4},{12,8},{16,12},{20,16},{24,20},{28,24},{5,1},{9,5},{13... | collective-permute-start | bytes 1179656 | tf_op jit(solution)/shard_map/ppermute | solution.py:22
  275.3 1.1 collective-permute-done.11
  276.5 53.8 %shard_map.102 = (f32[64,2048]{1,0:T(8,128)}, f32[64,2048]{1,0:T(8,128)S(1)}, f32[64,384]{1,0:T(8,128)S(1)}) custom-call(f32[64]{0:T(128)S(1)} %copy-done, f32[64]{0:T(128)S(1)} %mul.71.limit_ref, f32[64,5120]{1,0:T(8,128)S(1)} %pad_maximum_fusion.5.latent_in, f32[64,5120]{1,0:T(8,128)S(1)} %pad_maximum_fusion.4.proj_in, f32[64,512]{1,0:T(8,128)S(1)} %pad.40.taps_ref, ...), custom_call_target="tpu_custom_call" | custom-call | flops 2516582400 | bytes 2621440 | tf_op jit(solution)/shard_map/pallas_call | solution.py:171
  330.9 1.2 convolution_bitcast_fusion
  332.9 26.5 %shard_map.103 = f32[704,128]{1,0:T(8,128)S(1)} custom-call(f32[704,128]{1,0:T(8,128)S(1)} %pad_maximum_fusion.7.value_ref), custom_call_target="tpu_custom_call" | custom-call | flops 720896 | bytes 5767168 | tf_op jit(solution)/shard_map/pallas_call | solution.py:296
  361.2 1.0 fusion.49
  363.0 5.5 %shard_map.104 = f32[64,128]{1,0:T(8,128)S(1)} custom-call(f32[64,128]{1,0:T(8,128)S(1)} %pad.43.value_ref), custom_call_target="tpu_custom_call" | custom-call | flops 32768 | bytes 262144 | tf_op jit(solution)/shard_map/pallas_call | solution.py:296
  (109 shorter events, 20.8 us)
Async XLA Ops:
  0.6 6.5 %copy-start.3 = (f32[1024,64]{0,1:T(8,128)S(1)}, f32[1024,64]{0,1:T(8,128)}, u32[]{:S(2)}) copy-start(f32[1024,64]{0,1:T(8,128)} %param.8) | copy-start | bytes 786436
  10.3 21.4 %copy-start.4 = (f32[64,2048]{1,0:T(8,128)S(1)}, f32[64,2048]{1,0:T(8,128)}, u32[]{:S(2)}) copy-start(f32[64,2048]{1,0:T(8,128)} %param.10) | copy-start | bytes 1572868
  23.9 14.3 %copy-start.5 = (f32[64,256]{1,0:T(8,128)S(1)}, f32[64,256]{1,0:T(8,128)}, u32[]{:S(2)}) copy-start(f32[64,256]{1,0:T(8,128)} %param.9) | copy-start | bytes 196612
  24.9 15.1 %collective-permute-start.2 = (f32[64,1536]{1,0:T(8,128)}, f32[64,1536]{1,0:T(8,128)S(1)}, u32[]{:S(2)}, u32[]{:S(2)}) collective-permute-start(f32[64,1536]{1,0:T(8,128)} %get-tuple-element.42), channel_id=1, source_target_pairs={{0,4},{4,8},{8,12},{12,16},{16,20},{20,24},{24,28},{1,5},{5,9},{9,... | collective-permute-start | bytes 1179656 | tf_op jit(solution)/shard_map/ppermute | solution.py:22
  26.2 13.6 %copy-start = (f32[64]{0:T(128)S(1)}, f32[64]{0:T(128)}, u32[]{:S(2)}) copy-start(f32[64]{0:T(128)} %step_ref.7) | copy-start | bytes 772
  26.2 13.6 %copy-start.7 = (f32[64]{0:T(128)S(1)}, f32[64]{0:T(128)}, u32[]{:S(2)}) copy-start(f32[64]{0:T(128)} %param.11) | copy-start | bytes 772
  26.2 13.6 %copy-start.6 = (s32[16]{0:T(128)S(1)}, s32[16]{0:T(128)}, u32[]{:S(2)}) copy-start(s32[16]{0:T(128)} %param.13) | copy-start | bytes 196
  26.2 13.8 %collective-permute-start.3 = (f32[64,1536]{1,0:T(8,128)}, f32[64,1536]{1,0:T(8,128)S(1)}, u32[]{:S(2)}, u32[]{:S(2)}) collective-permute-start(f32[64,1536]{1,0:T(8,128)} %get-tuple-element.43), channel_id=1, source_target_pairs={{4,0},{8,4},{12,8},{16,12},{20,16},{24,20},{28,24},{5,1},{9,5},{13... | collective-permute-start | bytes 1179656 | tf_op jit(solution)/shard_map/ppermute | solution.py:22
  32.6 7.6 %collective-permute-start = (f32[64,1536]{1,0:T(8,128)}, f32[64,1536]{1,0:T(8,128)S(1)}, u32[]{:S(2)}, u32[]{:S(2)}) collective-permute-start(f32[64,1536]{1,0:T(8,128)} %get-tuple-element.44), channel_id=1, source_target_pairs={{0,4},{4,8},{8,12},{12,16},{16,20},{20,24},{24,28},{1,5},{5,9},{9,... | collective-permute-start | bytes 1179656 | tf_op jit(solution)/shard_map/ppermute | solution.py:22
  33.9 6.3 %collective-permute-start.1 = (f32[64,1536]{1,0:T(8,128)}, f32[64,1536]{1,0:T(8,128)S(1)}, u32[]{:S(2)}, u32[]{:S(2)}) collective-permute-start(f32[64,1536]{1,0:T(8,128)} %get-tuple-element.45), channel_id=1, source_target_pairs={{4,0},{8,4},{12,8},{16,12},{20,16},{24,20},{28,24},{5,1},{9,5},{13... | collective-permute-start | bytes 1179656 | tf_op jit(solution)/shard_map/ppermute | solution.py:22
  84.2 9.3 %collective-permute-start.4 = (f32[64,1536]{1,0:T(8,128)S(1)}, f32[64,1536]{1,0:T(8,128)S(1)}, u32[]{:S(2)}, u32[]{:S(2)}) collective-permute-start(f32[64,1536]{1,0:T(8,128)S(1)} %get-tuple-element.40), channel_id=1, source_target_pairs={{0,4},{4,8},{8,12},{12,16},{16,20},{20,24},{24,28},{1,5},{5,9},{9,... | collective-permute-start | bytes 1179656 | tf_op jit(solution)/shard_map/ppermute | solution.py:22
  85.5 9.2 %collective-permute-start.5 = (f32[64,1536]{1,0:T(8,128)S(1)}, f32[64,1536]{1,0:T(8,128)S(1)}, u32[]{:S(2)}, u32[]{:S(2)}) collective-permute-start(f32[64,1536]{1,0:T(8,128)S(1)} %get-tuple-element.41), channel_id=1, source_target_pairs={{4,0},{8,4},{12,8},{16,12},{20,16},{24,20},{28,24},{5,1},{9,5},{13... | collective-permute-start | bytes 1179656 | tf_op jit(solution)/shard_map/ppermute | solution.py:22
  94.8 54.4 %copy-start.1 = (bf16[1024,2048]{1,0:T(8,128)(2,1)S(1)}, bf16[1024,2048]{1,0:T(8,128)(2,1)}, u32[]{:S(2)}) copy-start(bf16[1024,2048]{1,0:T(8,128)(2,1)} %param.7) | copy-start | bytes 12582916
  206.0 14.3 %collective-permute-start.8 = (f32[64,1536]{1,0:T(8,128)}, f32[64,1536]{1,0:T(8,128)S(1)}, u32[]{:S(2)}, u32[]{:S(2)}) collective-permute-start(f32[64,1536]{1,0:T(8,128)} %get-tuple-element.34), channel_id=1, source_target_pairs={{0,4},{4,8},{8,12},{12,16},{16,20},{20,24},{24,28},{1,5},{5,9},{9,... | collective-permute-start | bytes 1179656 | tf_op jit(solution)/shard_map/ppermute | solution.py:22
  207.3 13.0 %collective-permute-start.9 = (f32[64,1536]{1,0:T(8,128)S(1)}, f32[64,1536]{1,0:T(8,128)S(1)}, u32[]{:S(2)}, u32[]{:S(2)}) collective-permute-start(f32[64,1536]{1,0:T(8,128)S(1)} %get-tuple-element.35), channel_id=1, source_target_pairs={{4,0},{8,4},{12,8},{16,12},{20,16},{24,20},{28,24},{5,1},{9,5},{13... | collective-permute-start | bytes 1179656 | tf_op jit(solution)/shard_map/ppermute | solution.py:22
  214.6 5.8 %collective-permute-start.6 = (f32[64,1536]{1,0:T(8,128)}, f32[64,1536]{1,0:T(8,128)S(1)}, u32[]{:S(2)}, u32[]{:S(2)}) collective-permute-start(f32[64,1536]{1,0:T(8,128)} %get-tuple-element.38), channel_id=1, source_target_pairs={{0,4},{4,8},{8,12},{12,16},{16,20},{20,24},{24,28},{1,5},{5,9},{9,... | collective-permute-start | bytes 1179656 | tf_op jit(solution)/shard_map/ppermute | solution.py:22
  215.9 5.6 %collective-permute-start.7 = (f32[64,1536]{1,0:T(8,128)S(1)}, f32[64,1536]{1,0:T(8,128)S(1)}, u32[]{:S(2)}, u32[]{:S(2)}) collective-permute-start(f32[64,1536]{1,0:T(8,128)S(1)} %get-tuple-element.39), channel_id=1, source_target_pairs={{4,0},{8,4},{12,8},{16,12},{20,16},{24,20},{28,24},{5,1},{9,5},{13... | collective-permute-start | bytes 1179656 | tf_op jit(solution)/shard_map/ppermute | solution.py:22
  265.5 9.8 %collective-permute-start.10 = (f32[64,1536]{1,0:T(8,128)S(1)}, f32[64,1536]{1,0:T(8,128)S(1)}, u32[]{:S(2)}, u32[]{:S(2)}) collective-permute-start(f32[64,1536]{1,0:T(8,128)S(1)} %get-tuple-element.32), channel_id=1, source_target_pairs={{0,4},{4,8},{8,12},{12,16},{16,20},{20,24},{24,28},{1,5},{5,9},{9,... | collective-permute-start | bytes 1179656 | tf_op jit(solution)/shard_map/ppermute | solution.py:22
  266.8 9.5 %collective-permute-start.11 = (f32[64,1536]{1,0:T(8,128)S(1)}, f32[64,1536]{1,0:T(8,128)S(1)}, u32[]{:S(2)}, u32[]{:S(2)}) collective-permute-start(f32[64,1536]{1,0:T(8,128)S(1)} %get-tuple-element.33), channel_id=1, source_target_pairs={{4,0},{8,4},{12,8},{16,12},{20,16},{24,20},{28,24},{5,1},{9,5},{13... | collective-permute-start | bytes 1179656 | tf_op jit(solution)/shard_map/ppermute | solution.py:22
  276.5 54.4 %copy-start.2 = (bf16[1024,2048]{1,0:T(8,128)(2,1)S(1)}, bf16[1024,2048]{1,0:T(8,128)(2,1)}, u32[]{:S(2)}) copy-start(bf16[1024,2048]{1,0:T(8,128)(2,1)} %param.7) | copy-start | bytes 12582916

commit v4 on v3

--- a/solution.py
+++ b/solution.py
@@ -14,12 +14,6 @@
 
 epsilon = 1e-06
 highest = lax.Precision.HIGHEST
-
-
-def passed_along(value, axis, steps):
-    count = lax.axis_size(axis)
-    leading, last = (max(0, -steps), min(count, count - steps))
-    return lax.ppermute(value, axis, [(source, source + steps) for source in range(leading, last)])
 
 
 def split3(matrix):
@@ -186,11 +180,64 @@
     )
 
 
-def widened(value):
+def widen_kernel(count, arrays, *refs):
+    values, outs = refs[:arrays], refs[arrays : 2 * arrays]
+    landed, send_sem, recv_sem = refs[2 * arrays :]
+    me = lax.axis_index("seg")
     rim = HALO * LANES
-    before = passed_along(value[:, value.shape[1] - rim :], "seg", 1)
-    after = passed_along(value[:, :rim], "seg", -1)
-    return jnp.concatenate([before, value, after], axis=1)
+    own = values[0].shape[1]
+    after, before = lax.rem(me + 1, count), lax.rem(me + count - 1, count)
+    barrier = pltpu.get_barrier_semaphore()
+    for peer in (after, before):
+        pl.semaphore_signal(
+            barrier, inc=1, device_id={"seg": peer}, device_id_type=pl.DeviceIdType.MESH
+        )
+    pl.semaphore_wait(barrier, 2)
+    copies = []
+    for index in range(arrays):
+        for side, peer, first in ((0, after, own - rim), (1, before, 0)):
+            copy = pltpu.make_async_remote_copy(
+                src_ref=values[index].at[:, pl.ds(first, rim)],
+                dst_ref=landed.at[index, side],
+                send_sem=send_sem.at[index, side],
+                recv_sem=recv_sem.at[index, side],
+                device_id={"seg": peer},
+                device_id_type=pl.DeviceIdType.MESH,
+            )
+            copy.start()
+            copies.append(copy)
+    for index in range(arrays):
+        outs[index][:, rim : rim + own] = values[index][...]
+    for copy in copies:
+        copy.wait()
+    for index in range(arrays):
+        outs[index][:, :rim] = jnp.where(me > 0, landed[index, 0], 0.0)
+        outs[index][:, rim + own :] = jnp.where(me < count - 1, landed[index, 1], 0.0)
+
+
+def widened(*values):
+    count = lax.axis_size("seg")
+    arrays = len(values)
+    rows, own = values[0].shape
+    rim = HALO * LANES
+    in_vmem = pl.BlockSpec(memory_space=pltpu.VMEM)
+    return pl.pallas_call(
+        functools.partial(widen_kernel, count, arrays),
+        out_shape=[jax.ShapeDtypeStruct((rows, own + 2 * rim), jnp.float32)] * arrays,
+        in_specs=[in_vmem] * arrays,
+        out_specs=[in_vmem] * arrays,
+        scratch_shapes=[
+            pltpu.VMEM((arrays, 2, rows, rim), jnp.float32),
+            pltpu.SemaphoreType.DMA((arrays, 2)),
+            pltpu.SemaphoreType.DMA((arrays, 2)),
+        ],
+        compiler_params=pltpu.CompilerParams(
+            collective_id=3 + arrays, has_side_effects=True, vmem_limit_bytes=24 * 1024 * 1024
+        ),
+        cost_estimate=pl.CostEstimate(
+            flops=0, bytes_accessed=24 * arrays * rows * own, transcendentals=0
+        ),
+    )(*values)
 
 
 def whole_sum_kernel(axis, count, value_ref, out_ref, landed, send_sem, recv_sem):
@@ -367,13 +414,14 @@
         space_b = space_loc.astype(jnp.bfloat16)
         kernel_b = kernel.astype(jnp.bfloat16)
         projected = projected_sum(space_b, signal)
-        wide = widened(projected)
+        latent_wide, wide = widened(latent, projected)
         (latent,) = run_steps(
-            ITERS // 2, False, widened(latent), wide, kernel_b, gram_matrix,
+            ITERS // 2, False, latent_wide, wide, kernel_b, gram_matrix,
             step_sizes, limits, allowed, inside,
         )
+        (latent_wide,) = widened(latent)
         latent, rebuilt, lags = run_steps(
-            ITERS - ITERS // 2, True, widened(latent), wide, kernel_b, gram_matrix,
+            ITERS - ITERS // 2, True, latent_wide, wide, kernel_b, gram_matrix,
             step_sizes, limits, allowed, inside,
         )
         taps_part = lags[:, 1 : tap_count + 1][:, ::-1]

time: 371 us -> 380 us (1.024)
  Pallas kernels: 292 us -> 349 us
  starting transfers between devices: 41.9 us -> 0 us
  local copies, waits for them, and re-layouts: 13.5 us -> 8.3 us
    pallas_call x0 -> x4, Pallas kernels: none -> 65.4 us  [widened(): pl.pallas_call(functools.partial(widen_kernel, count, arrays), out_shape=...]
    ppermute x12 -> x0, starting transfers between devices: 41.9 us -> none  [passed_along(): lax.ppermute(value, axis, [(source, source + steps) for source in range(l...]
    pallas_call x7, Pallas kernels: 96.4 us -> 88 us  [device_sum(): pl.pallas_call(functools.partial(kernel, axis, count), out_shape=jax.Shap...]
  transfers between devices with their start and end apart: 12 -> 0, of which waited for: 3 -> 0; matrix products, arithmetic and copies ran while one was open for 2% -> 0% of each run, Pallas kernels for 0% -> 0%
where the time goes in v4:
time: 380 us; the launch traced here: 379 us
  Pallas kernels  349 us (92%)
  matrix products  15 us (4%)
  local copies, waits for them, and re-layouts  8.3 us (2%)
  other arithmetic  5.97 us (2%)
    pallas_call x4, Pallas kernels, run_steps(): pl.pallas_call(functools.partial(steps_kernel, steps, last, atoms, blocks...  196 us
    pallas_call x7, Pallas kernels, device_sum(): pl.pallas_call(functools.partial(kernel, axis, count), out_shape=jax.Shap...  88 us
    pallas_call x4, Pallas kernels, widened(): pl.pallas_call(functools.partial(widen_kernel, count, arrays), out_shape=...  65.4 us

profile of v4, /device:TPU:25, one launch (start us, length us, event | category | flops | bytes accessed | tf_op | source)
XLA Modules:
  0.0 379.3 jit_solution(3911504108722805325)
XLA Ops:
  1.3 0.9 multiply_reduce_fusion.2
  2.3 1.4 fusion.39
  3.7 4.2 %shard_map.94 = f32[64,128]{1,0:T(8,128)S(1)} custom-call(f32[64,128]{1,0:T(8,128)S(1)} %pad.35.value_ref), custom_call_target="tpu_custom_call" | custom-call | flops 32768 | bytes 262144 | tf_op jit(solution)/shard_map/pallas_call | solution.py:343
  8.0 0.8 gather_fusion
  8.9 0.8 gather_fusion.1
  9.9 0.8 and_reduce_fusion
  10.7 0.9 fusion.10
  11.9 3.2 fusion.7.value_ref
  15.1 15.1 %shard_map.95.refs_1_ = f32[64,2048]{1,0:T(8,128)S(1)} custom-call(f32[64,2048]{1,0:T(8,128)S(1)} %fusion.7.value_ref), custom_call_target="tpu_custom_call" | custom-call | flops 524288 | bytes 4194304 | tf_op jit(solution)/shard_map/pallas_call | solution.py:343
  30.2 20.5 %shard_map.96 = (f32[64,5120]{1,0:T(8,128)S(1)}, f32[64,5120]{1,0:T(8,128)S(1)}) custom-call(f32[64,2048]{1,0:T(8,128)S(1)} %copy-done, f32[64,2048]{1,0:T(8,128)S(1)} %shard_map.95.refs_1_), custom_call_target="tpu_custom_call" | custom-call | bytes 6291456 | tf_op jit(solution)/shard_map/pallas_call | solution.py:224
  50.8 43.8 %shard_map.97.refs_0_ = f32[64,2048]{1,0:T(8,128)S(1)} custom-call(f32[64]{0:T(128)S(1)} %copy-done.1, f32[64]{0:T(128)S(1)} %mul.71.limit_ref, f32[64,5120]{1,0:T(8,128)S(1)} %get-tuple-element.13.latent_in, f32[64,5120]{1,0:T(8,128)S(1)} %get-tuple-element.14.proj_in, f32[64,512]{1,0:T(8,128)S(1)} %pad.36.taps_ref, f32[64,512]{1,0:T(8,128)S(1)} %pad.37.flipped_ref, ...), custom_call_target="tpu_custom_call" | custom-call | flops 2516582400 | bytes 2621440 | tf_op jit(solution)/shard_map/pallas_call | solution.py:165
  94.7 12.0 %shard_map.98.latent_in = f32[64,5120]{1,0:T(8,128)S(1)} custom-call(f32[64,2048]{1,0:T(8,128)S(1)} %shard_map.97.refs_0_), custom_call_target="tpu_custom_call" | custom-call | bytes 3145728 | tf_op jit(solution)/shard_map/pallas_call | solution.py:224
  106.7 53.8 %shard_map.99 = (f32[64,2048]{1,0:T(8,128)S(1)}, f32[64,2048]{1,0:T(8,128)S(1)}, f32[64,384]{1,0:T(8,128)S(1)}) custom-call(f32[64]{0:T(128)S(1)} %copy-done.1, f32[64]{0:T(128)S(1)} %mul.71.limit_ref, f32[64,5120]{1,0:T(8,128)S(1)} %shard_map.98.latent_in, f32[64,5120]{1,0:T(8,128)S(1)} %get-tuple-element.14.proj_in, f32[64,512]{1,0:T(8,128)S(1)} %pad.36.taps_ref, ...), custom_call_target="tpu_custom_call" | custom-call | flops 2516582400 | bytes 2621440 | tf_op jit(solution)/shard_map/pallas_call | solution.py:165
  161.1 1.2 convolution_bitcast_fusion.1
  163.1 21.7 %shard_map.100 = f32[704,128]{1,0:T(8,128)S(1)} custom-call(f32[704,128]{1,0:T(8,128)S(1)} %pad_maximum_fusion.value_ref), custom_call_target="tpu_custom_call" | custom-call | flops 720896 | bytes 5767168 | tf_op jit(solution)/shard_map/pallas_call | solution.py:343
  184.9 0.8 gather_fusion.2
  186.4 1.1 convolution_subtract_fusion
  187.5 1.0 fusion.41
  188.6 5.8 %shard_map.101 = f32[64,128]{1,0:T(8,128)S(1)} custom-call(f32[64,128]{1,0:T(8,128)S(1)} %pad.39.value_ref), custom_call_target="tpu_custom_call" | custom-call | flops 32768 | bytes 262144 | tf_op jit(solution)/shard_map/pallas_call | solution.py:343
  194.4 0.8 gather_fusion.3
  195.4 0.8 gather_fusion.4
  196.4 3.1 fusion.1.value_ref
  199.4 14.3 %shard_map.102.refs_1_ = f32[64,2048]{1,0:T(8,128)S(1)} custom-call(f32[64,2048]{1,0:T(8,128)S(1)} %fusion.1.value_ref), custom_call_target="tpu_custom_call" | custom-call | flops 524288 | bytes 4194304 | tf_op jit(solution)/shard_map/pallas_call | solution.py:343
  213.8 19.7 %shard_map.103 = (f32[64,5120]{1,0:T(8,128)S(1)}, f32[64,5120]{1,0:T(8,128)S(1)}) custom-call(f32[64,2048]{1,0:T(8,128)S(1)} %get-tuple-element.15.refs_0_, f32[64,2048]{1,0:T(8,128)S(1)} %shard_map.102.refs_1_), custom_call_target="tpu_custom_call" | custom-call | bytes 6291456 | tf_op jit(solution)/shard_map/pallas_call | solution.py:224
  233.5 44.0 %shard_map.104.refs_0_ = f32[64,2048]{1,0:T(8,128)S(1)} custom-call(f32[64]{0:T(128)S(1)} %copy-done.1, f32[64]{0:T(128)S(1)} %mul.71.limit_ref, f32[64,5120]{1,0:T(8,128)S(1)} %get-tuple-element.18.latent_in, f32[64,5120]{1,0:T(8,128)S(1)} %get-tuple-element.19.proj_in, f32[64,512]{1,0:T(8,128)S(1)} %pad.40.taps_ref, f32[64,512]{1,0:T(8,128)S(1)} %pad.41.flipped_ref, ...), custom_call_target="tpu_custom_call" | custom-call | flops 2516582400 | bytes 2621440 | tf_op jit(solution)/shard_map/pallas_call | solution.py:165
  277.5 13.1 %shard_map.105.latent_in = f32[64,5120]{1,0:T(8,128)S(1)} custom-call(f32[64,2048]{1,0:T(8,128)S(1)} %shard_map.104.refs_0_), custom_call_target="tpu_custom_call" | custom-call | bytes 3145728 | tf_op jit(solution)/shard_map/pallas_call | solution.py:224
  290.7 53.8 %shard_map.106 = (f32[64,2048]{1,0:T(8,128)}, f32[64,2048]{1,0:T(8,128)S(1)}, f32[64,384]{1,0:T(8,128)S(1)}) custom-call(f32[64]{0:T(128)S(1)} %copy-done.1, f32[64]{0:T(128)S(1)} %mul.71.limit_ref, f32[64,5120]{1,0:T(8,128)S(1)} %shard_map.105.latent_in, f32[64,5120]{1,0:T(8,128)S(1)} %get-tuple-element.19.proj_in, f32[64,512]{1,0:T(8,128)S(1)} %pad.40.taps_ref, ...), custom_call_target="tpu_custom_call" | custom-call | flops 2516582400 | bytes 2621440 | tf_op jit(solution)/shard_map/pallas_call | solution.py:165
  345.1 1.2 convolution_bitcast_fusion
  347.1 21.2 %shard_map.107 = f32[704,128]{1,0:T(8,128)S(1)} custom-call(f32[704,128]{1,0:T(8,128)S(1)} %pad_maximum_fusion.1.value_ref), custom_call_target="tpu_custom_call" | custom-call | flops 720896 | bytes 5767168 | tf_op jit(solution)/shard_map/pallas_call | solution.py:343
  370.9 1.0 fusion.43
  372.0 5.6 %shard_map.108 = f32[64,128]{1,0:T(8,128)S(1)} custom-call(f32[64,128]{1,0:T(8,128)S(1)} %pad.43.value_ref), custom_call_target="tpu_custom_call" | custom-call | flops 32768 | bytes 262144 | tf_op jit(solution)/shard_map/pallas_call | solution.py:343
  378.4 0.9 copy.24
  (71 shorter events, 8.4 us)
Async XLA Ops:
  3.7 26.5 %copy-start = (f32[64,2048]{1,0:T(8,128)S(1)}, f32[64,2048]{1,0:T(8,128)}, u32[]{:S(2)}) copy-start(f32[64,2048]{1,0:T(8,128)} %refs_0_.1) | copy-start | bytes 1572868
  8.9 41.9 %copy-start.1 = (f32[64]{0:T(128)S(1)}, f32[64]{0:T(128)}, u32[]{:S(2)}) copy-start(f32[64]{0:T(128)} %step_ref.7) | copy-start | bytes 772
  106.6 54.4 %copy-start.2 = (bf16[1024,2048]{1,0:T(8,128)(2,1)S(1)}, bf16[1024,2048]{1,0:T(8,128)(2,1)}, u32[]{:S(2)}) copy-start(bf16[1024,2048]{1,0:T(8,128)(2,1)} %param.7) | copy-start | bytes 12582916
  162.3 24.1 %copy-start.4 = (f32[1024,64]{0,1:T(8,128)S(1)}, f32[1024,64]{0,1:T(8,128)}, u32[]{:S(2)}) copy-start(f32[1024,64]{0,1:T(8,128)} %param.8) | copy-start | bytes 786436
  290.7 54.4 %copy-start.3 = (bf16[1024,2048]{1,0:T(8,128)(2,1)S(1)}, bf16[1024,2048]{1,0:T(8,128)(2,1)}, u32[]{:S(2)}) copy-start(bf16[1024,2048]{1,0:T(8,128)(2,1)} %param.7) | copy-start | bytes 12582916
